TPU v7x, 32 devices: a whole 2x2x4 slice. The times are simulated.
32 devices in a mesh: groups: 2 (over x), lon: 16 (over z, y, core).
Axes of the slice: x: 2, y: 2, z: 4, core: 2. Of those that a mesh axis runs over, the one named last changes fastest.
Arguments:
- source: bfloat16 [32, 1024, 256], P('groups', 'lon'), parts along dimension 0, may hold values from -6 to 6
- quadrature: bfloat16 [9, 16, 6, 64], replicated, may hold values from -0.29882812 to 0.29882812
- block_rows: int32 [16, 6], replicated, may hold values from 0 to 15, as said below
- offsets: int32 [16, 6], replicated, may hold values from -64 to 0
- counts: int32 [16], replicated, may hold values from 1 to 6, as said below
- weight: bfloat16 [9, 256, 256], replicated, may hold values from -0.125 to 0.125
- cotangent: bfloat16 [32, 1024, 256], P('groups', 'lon'), parts along dimension 0, may hold values from -6 to 6
Outputs:
- mixed: bfloat16 [32, 1024, 256], P('groups', 'lon'), parts along dimension 0
- grad_source: float32 [32, 1024, 256], P('groups', 'lon'), parts along dimension 0
- grad_weight: float32 [18, 256, 256], P('groups'), parts along dimension 0
There are 2 independent parts, one for each index of `groups`. A program takes and returns all parts, laid end to end along the dimension named above; an argument that names none is the same for every part. Nothing has to cross between parts.
Inputs may be any that keep to these rules, and one draw needn't show every extreme that they name: `block_rows`: within 3 rows of the output row. `counts`: blocks at or past the count are ignored.
All inputs are finite; a program needn't handle non-finite values.
Results may differ from a plain program's by a relative error of at most 0.0049.
Values may be sent and summed in bfloat16 or wider, within the bound.
A program may use at most 128 MiB of HBM per device.

v0:
```python
import math

import jax
import jax.numpy as jnp
from jax import lax
from jax.sharding import PartitionSpec as P

row_reach = 3


def padded(array, sides, width):
    for axis, dim in sides:
        peers, length = (lax.axis_size(axis), array.shape[dim])
        up = [(i, (i + 1) % peers) for i in range(peers)]
        down = [(j, i) for i, j in up]
        last = lax.slice_in_dim(array, length - width, length, axis=dim)
        leading = lax.slice_in_dim(array, 0, width, axis=dim)
        before = lax.ppermute(last, axis, up)
        after = lax.ppermute(leading, axis, down)
        array = jnp.concatenate([before, array, after], axis=dim)
    return array


def from_behind(array, axis, by):
    peers = lax.axis_size(axis)
    return lax.ppermute(array, axis, [(i, (i + by) % peers) for i in range(peers)])


def banded(quad_row, live_row, placed, rows_a, cols_c, stencil):
    span = rows_a + cols_c - 1
    spots = jnp.arange(span, dtype=jnp.int32)
    tap_ids = jnp.arange(stencil, dtype=jnp.int32)
    matches = (spots[None, :, None] - placed[:, None, None] == tap_ids[None, None, :]).astype(
        jnp.bfloat16
    )
    scaled = jnp.where(live_row[None, :, None], quad_row, jnp.zeros((), quad_row.dtype))
    profile = jnp.einsum(
        "kbt,but->kbu", scaled, matches, preferred_element_type=jnp.float32
    ).astype(jnp.bfloat16)
    profile = jnp.roll(profile, -(rows_a - 1), axis=2)
    filters, blocks = (profile.shape[0], profile.shape[1])
    repeated = jnp.tile(profile, (1, 1, rows_a))[:, :, : rows_a * (span - 1)]
    return repeated.reshape(filters, blocks, rows_a, span - 1)[:, :, :, :cols_c]


def shards(source, quadrature, block_rows, offsets, counts, weight, cotangent):
    lat_rows, columns_here, channels = source.shape
    filters = weight.shape[0]
    blocks = block_rows.shape[1]
    stencil = quadrature.shape[3]
    padded_width = columns_here + 2 * stencil
    stack_rows = 2 * row_reach + 1
    lon_devices = lax.axis_size("lon")
    extended = padded(source, (("lon", 1),), stencil)
    lat_padded = jnp.pad(extended, ((row_reach, row_reach), (0, 0), (0, 0)))
    alive = jnp.arange(blocks, dtype=jnp.int32)[None, :] < counts[:, None]
    stack_ids = jnp.arange(stack_rows, dtype=jnp.int32)
    mix_matrix = weight.reshape(filters * channels, channels)
    flat_grad = cotangent.reshape(lat_rows * columns_here, channels)
    grad_basis = lax.dot_general(
        flat_grad, mix_matrix, (((1,), (1,)), ((), ())), preferred_element_type=jnp.float32
    ).astype(jnp.bfloat16)
    grad_basis = grad_basis.reshape(lat_rows, columns_here, filters, channels)

    def step_row(i, carry):
        basis, total = carry
        quad_row = lax.dynamic_index_in_dim(quadrature, i, 1, keepdims=False)
        live_row = alive[i]
        relative = block_rows[i] - i + row_reach
        selector = (relative[:, None] == stack_ids[None, :]).astype(jnp.bfloat16)
        stacked = lax.dynamic_slice(lat_padded, (i, 0, 0), (stack_rows, padded_width, channels))
        selected = jnp.einsum(
            "bd,dwc->bwc", selector, stacked, preferred_element_type=jnp.float32
        ).astype(jnp.bfloat16)
        forward_band = banded(
            quad_row,
            live_row,
            columns_here - 1 + stencil + offsets[i],
            columns_here,
            padded_width,
            stencil,
        )
        basis_row = jnp.einsum(
            "kbjw,bwc->jkc", forward_band, selected, preferred_element_type=jnp.float32
        ).astype(jnp.bfloat16)
        basis = lax.dynamic_update_slice(basis, basis_row[None], (i, 0, 0, 0))
        grad_row = lax.dynamic_index_in_dim(grad_basis, i, 0, keepdims=False)
        pieces = jnp.einsum(
            "kbjw,jkc->bwc", forward_band, grad_row, preferred_element_type=jnp.float32
        )
        spread = jnp.einsum(
            "bd,bwc->dwc",
            selector.astype(jnp.float32),
            pieces,
            precision=lax.Precision.HIGHEST,
            preferred_element_type=jnp.float32,
        )
        current = lax.dynamic_slice(total, (i, 0, 0), (stack_rows, padded_width, channels))
        total = lax.dynamic_update_slice(total, current + spread, (i, 0, 0))
        return (basis, total)

    basis_init = jnp.zeros((lat_rows, columns_here, filters, channels), jnp.bfloat16)
    total_init = jnp.zeros((lat_rows + 2 * row_reach, padded_width, channels), jnp.float32)
    basis, total = lax.fori_loop(0, lat_rows, step_row, (basis_init, total_init))
    accumulated = total[row_reach : row_reach + lat_rows]
    flat_basis = basis.reshape(lat_rows * columns_here, filters * channels)
    mixed = jnp.dot(flat_basis, mix_matrix, preferred_element_type=jnp.float32).astype(jnp.bfloat16)
    mixed = mixed.reshape(lat_rows, columns_here, channels)
    factor = 1.0 / math.sqrt(lat_rows * columns_here * lon_devices)
    local_grad = lax.dot_general(
        flat_basis, flat_grad, (((0,), (0,)), ((), ())), preferred_element_type=jnp.float32
    )
    summed = lax.psum(local_grad, "lon")
    grad_weight = (summed * factor).reshape(filters, channels, channels)
    west_rim = accumulated[:, :stencil]
    east_rim = accumulated[:, columns_here + stencil :]
    west_incoming = from_behind(east_rim.astype(jnp.bfloat16), "lon", 1).astype(east_rim.dtype)
    east_incoming = from_behind(west_rim.astype(jnp.bfloat16), "lon", -1).astype(west_rim.dtype)
    interior = accumulated[:, stencil : stencil + columns_here]
    interior = interior.at[:, :stencil].add(west_incoming)
    grad_source = interior.at[:, columns_here - stencil :].add(east_incoming)
    return (mixed, grad_source, grad_weight)


def solution(mesh):
    return jax.shard_map(
        shards,
        mesh=mesh,
        in_specs=(P("groups", "lon", None), P(), P(), P(), P(), P(), P("groups", "lon", None)),
        out_specs=(P("groups", "lon", None), P("groups", "lon", None), P("groups", None, None)),
        check_vma=False,
    )
```

profile of v0, /device:TPU:29, one launch (start us, length us, event | category | flops | bytes accessed | tf_op | source)
XLA Modules:
  0.0 618.9 jit_solution(18108099271244288832)
XLA Ops:
  15.9 10.2 %reshape.151 = bf16[16,64,9,256]{3,2,1,0:T(8,128)(2,1)} reshape(bf16[1024,2304]{1,0:T(8,128)(2,1)} %convolution_convert_fusion.1) | data formatting | bytes 9437184 | tf_op jit(solution)/shard_map/reshape | solution.py:63
  31.0 461.8 %while.20 = (s32[]{:T(128)}, bf16[16,64,9,256]{3,1,2,0:T(8,128)(2,1)}, f32[22,192,256]{2,1,0:T(8,128)}, s32[16,6]{1,0:T(8,128)S(1)}, bf16[22,192,256]{2,1,0:T(8,...) while((s32[]{:T(128)}, ...), condition=%wide.region_1.2_spmd.clone, body=%wide.region_0.1_spmd.clone.sunk | while | flops 710804544 | bytes 57469300 | solution.py:104
  45.9 6.9 %reshape.162 = bf16[9,6,64,254]{3,2,1,0:T(8,128)(2,1)S(1)} reshape(bf16[9,6,16256]{2,1,0:T(8,128)(2,1)} %slice.120) | data formatting | bytes 3511296 | tf_op jit(solution)/shard_map/while/body/eval_jaxpr/reshape | solution.py:43
  74.7 6.9 %reshape.162 = bf16[9,6,64,254]{3,2,1,0:T(8,128)(2,1)S(1)} reshape(bf16[9,6,16256]{2,1,0:T(8,128)(2,1)} %slice.120) | data formatting | bytes 3511296 | tf_op jit(solution)/shard_map/while/body/eval_jaxpr/reshape | solution.py:43
  97.4 4.7 tile.26
  103.6 6.9 %reshape.162 = bf16[9,6,64,254]{3,2,1,0:T(8,128)(2,1)S(1)} reshape(bf16[9,6,16256]{2,1,0:T(8,128)(2,1)} %slice.120) | data formatting | bytes 3511296 | tf_op jit(solution)/shard_map/while/body/eval_jaxpr/reshape | solution.py:43
  132.5 6.9 %reshape.162 = bf16[9,6,64,254]{3,2,1,0:T(8,128)(2,1)S(1)} reshape(bf16[9,6,16256]{2,1,0:T(8,128)(2,1)} %slice.120) | data formatting | bytes 3511296 | tf_op jit(solution)/shard_map/while/body/eval_jaxpr/reshape | solution.py:43
  161.3 6.9 %reshape.162 = bf16[9,6,64,254]{3,2,1,0:T(8,128)(2,1)S(1)} reshape(bf16[9,6,16256]{2,1,0:T(8,128)(2,1)} %slice.120) | data formatting | bytes 3511296 | tf_op jit(solution)/shard_map/while/body/eval_jaxpr/reshape | solution.py:43
  190.2 6.9 %reshape.162 = bf16[9,6,64,254]{3,2,1,0:T(8,128)(2,1)S(1)} reshape(bf16[9,6,16256]{2,1,0:T(8,128)(2,1)} %slice.120) | data formatting | bytes 3511296 | tf_op jit(solution)/shard_map/while/body/eval_jaxpr/reshape | solution.py:43
  219.1 6.9 %reshape.162 = bf16[9,6,64,254]{3,2,1,0:T(8,128)(2,1)S(1)} reshape(bf16[9,6,16256]{2,1,0:T(8,128)(2,1)} %slice.120) | data formatting | bytes 3511296 | tf_op jit(solution)/shard_map/while/body/eval_jaxpr/reshape | solution.py:43
  241.7 4.7 tile.26
  247.9 6.9 %reshape.162 = bf16[9,6,64,254]{3,2,1,0:T(8,128)(2,1)S(1)} reshape(bf16[9,6,16256]{2,1,0:T(8,128)(2,1)} %slice.120) | data formatting | bytes 3511296 | tf_op jit(solution)/shard_map/while/body/eval_jaxpr/reshape | solution.py:43
  276.8 6.9 %reshape.162 = bf16[9,6,64,254]{3,2,1,0:T(8,128)(2,1)S(1)} reshape(bf16[9,6,16256]{2,1,0:T(8,128)(2,1)} %slice.120) | data formatting | bytes 3511296 | tf_op jit(solution)/shard_map/while/body/eval_jaxpr/reshape | solution.py:43
  305.7 6.9 %reshape.162 = bf16[9,6,64,254]{3,2,1,0:T(8,128)(2,1)S(1)} reshape(bf16[9,6,16256]{2,1,0:T(8,128)(2,1)} %slice.120) | data formatting | bytes 3511296 | tf_op jit(solution)/shard_map/while/body/eval_jaxpr/reshape | solution.py:43
  328.2 4.7 tile.26
  334.5 6.9 %reshape.162 = bf16[9,6,64,254]{3,2,1,0:T(8,128)(2,1)S(1)} reshape(bf16[9,6,16256]{2,1,0:T(8,128)(2,1)} %slice.120) | data formatting | bytes 3511296 | tf_op jit(solution)/shard_map/while/body/eval_jaxpr/reshape | solution.py:43
  363.3 6.9 %reshape.162 = bf16[9,6,64,254]{3,2,1,0:T(8,128)(2,1)S(1)} reshape(bf16[9,6,16256]{2,1,0:T(8,128)(2,1)} %slice.120) | data formatting | bytes 3511296 | tf_op jit(solution)/shard_map/while/body/eval_jaxpr/reshape | solution.py:43
  392.2 6.9 %reshape.162 = bf16[9,6,64,254]{3,2,1,0:T(8,128)(2,1)S(1)} reshape(bf16[9,6,16256]{2,1,0:T(8,128)(2,1)} %slice.120) | data formatting | bytes 3511296 | tf_op jit(solution)/shard_map/while/body/eval_jaxpr/reshape | solution.py:43
  421.0 6.9 %reshape.162 = bf16[9,6,64,254]{3,2,1,0:T(8,128)(2,1)S(1)} reshape(bf16[9,6,16256]{2,1,0:T(8,128)(2,1)} %slice.120) | data formatting | bytes 3511296 | tf_op jit(solution)/shard_map/while/body/eval_jaxpr/reshape | solution.py:43
  449.9 6.9 %reshape.162 = bf16[9,6,64,254]{3,2,1,0:T(8,128)(2,1)S(1)} reshape(bf16[9,6,16256]{2,1,0:T(8,128)(2,1)} %slice.120) | data formatting | bytes 3511296 | tf_op jit(solution)/shard_map/while/body/eval_jaxpr/reshape | solution.py:43
  478.8 6.9 %reshape.162 = bf16[9,6,64,254]{3,2,1,0:T(8,128)(2,1)S(1)} reshape(bf16[9,6,16256]{2,1,0:T(8,128)(2,1)} %slice.120) | data formatting | bytes 3511296 | tf_op jit(solution)/shard_map/while/body/eval_jaxpr/reshape | solution.py:43
  492.8 6.2 copy.20
  516.0 10.8 %collective-permute-done.2 = bf16[16,64,256]{2,1,0:T(8,128)(2,1)S(1)} collective-permute-done((bf16[16,64,256]{2,1,0:T(8,128)(2,1)S(1)}, bf16[16,64,256]{2,1,0:T(8,128)(2,1)S(1)}, u32[]{:S(2)}, u32[]{:S(2)}) %collective-permute-start.2) | collective-permute-done | bytes 524320 | tf_op jit(solution)/shard_map/ppermute | solution.py:26
  531.9 76.9 %all-reduce.3.cloned.1.call-done = f32[2304,256]{1,0:T(8,128)} async-done(((f32[2304,256]{1,0:T(8,128)}), f32[2304,256]{1,0:T(8,128)}) %all-reduce.3.cloned.1.call-update) | async-done | bytes 2359312 | tf_op jit(solution)/shard_map/psum | solution.py:113
  (564 shorter events, 373.9 us)
Async XLA Ops:
  7.2 601.7 %all-reduce.3.cloned.1.call-start = ((), (), s32[]{:S(2)}) async-start(), calls=%async_computation | async-start | bytes 4718592 | tf_op jit(solution)/shard_map/psum | solution.py:113
  7.2 19.0 %collective-permute-start = (bf16[16,64,256]{2,1,0:T(8,128)(2,1)}, bf16[16,64,256]{2,1,0:T(8,128)(2,1)S(1)}, u32[]{:S(2)}, u32[]{:S(2)}) collective-permute-start(bf16[16,64,256]{2,1,0:T(8,128)(2,1)} %param.17), channel_id=1, source_target_pairs={{0,1},{1,2},{2,3},{3,4},{4,5},{5,6},{6,7},{7,8},{8,9},{9,10},{10,1... | collective-permute-start | bytes 1572872 | tf_op jit(solution)/shard_map/ppermute | solution.py:18
  7.3 19.7 %collective-permute-start.1 = (bf16[16,64,256]{2,1,0:T(8,128)(2,1)}, bf16[16,64,256]{2,1,0:T(8,128)(2,1)}, u32[]{:S(2)}, u32[]{:S(2)}) collective-permute-start(bf16[16,64,256]{2,1,0:T(8,128)(2,1)} %param.17), channel_id=1, source_target_pairs={{1,0},{2,1},{3,2},{4,3},{5,4},{6,5},{7,6},{8,7},{9,8},{10,9},{11,1... | collective-permute-start | bytes 1572872 | tf_op jit(solution)/shard_map/ppermute | solution.py:19
  15.9 10.2 %copy-start.11 = (s32[16]{0:T(128)S(1)}, s32[16]{0:T(128)}, u32[]{:S(2)}) copy-start(s32[16]{0:T(128)} %param.21) | copy-start | bytes 196
  88.8 7.2 %copy-start.9 = (s32[16,6]{1,0:T(8,128)}, s32[16,6]{1,0:T(8,128)S(1)}, u32[]{:S(2)}) copy-start(s32[16,6]{1,0:T(8,128)S(1)} %get-tuple-element.359) | copy-start | bytes 1156 | tf_op jit(solution)/shard_map/while
  117.6 7.2 %copy-start.3 = (bf16[22,192,256]{2,1,0:T(8,128)(2,1)}, bf16[22,192,256]{2,1,0:T(8,128)(2,1)S(1)}, u32[]{:S(2)}) copy-start(bf16[22,192,256]{2,1,0:T(8,128)(2,1)S(1)} %get-tuple-element.358) | copy-start | bytes 6488068 | tf_op jit(solution)/shard_map/while
  117.6 7.2 %copy-start.9 = (s32[16,6]{1,0:T(8,128)}, s32[16,6]{1,0:T(8,128)S(1)}, u32[]{:S(2)}) copy-start(s32[16,6]{1,0:T(8,128)S(1)} %get-tuple-element.359) | copy-start | bytes 1156 | tf_op jit(solution)/shard_map/while
  146.5 7.2 %copy-start.3 = (bf16[22,192,256]{2,1,0:T(8,128)(2,1)}, bf16[22,192,256]{2,1,0:T(8,128)(2,1)S(1)}, u32[]{:S(2)}) copy-start(bf16[22,192,256]{2,1,0:T(8,128)(2,1)S(1)} %get-tuple-element.358) | copy-start | bytes 6488068 | tf_op jit(solution)/shard_map/while
  146.5 7.2 %copy-start.9 = (s32[16,6]{1,0:T(8,128)}, s32[16,6]{1,0:T(8,128)S(1)}, u32[]{:S(2)}) copy-start(s32[16,6]{1,0:T(8,128)S(1)} %get-tuple-element.359) | copy-start | bytes 1156 | tf_op jit(solution)/shard_map/while
  175.4 7.2 %copy-start.3 = (bf16[22,192,256]{2,1,0:T(8,128)(2,1)}, bf16[22,192,256]{2,1,0:T(8,128)(2,1)S(1)}, u32[]{:S(2)}) copy-start(bf16[22,192,256]{2,1,0:T(8,128)(2,1)S(1)} %get-tuple-element.358) | copy-start | bytes 6488068 | tf_op jit(solution)/shard_map/while
  175.4 7.2 %copy-start.9 = (s32[16,6]{1,0:T(8,128)}, s32[16,6]{1,0:T(8,128)S(1)}, u32[]{:S(2)}) copy-start(s32[16,6]{1,0:T(8,128)S(1)} %get-tuple-element.359) | copy-start | bytes 1156 | tf_op jit(solution)/shard_map/while
  204.2 7.2 %copy-start.3 = (bf16[22,192,256]{2,1,0:T(8,128)(2,1)}, bf16[22,192,256]{2,1,0:T(8,128)(2,1)S(1)}, u32[]{:S(2)}) copy-start(bf16[22,192,256]{2,1,0:T(8,128)(2,1)S(1)} %get-tuple-element.358) | copy-start | bytes 6488068 | tf_op jit(solution)/shard_map/while
  204.2 7.2 %copy-start.9 = (s32[16,6]{1,0:T(8,128)}, s32[16,6]{1,0:T(8,128)S(1)}, u32[]{:S(2)}) copy-start(s32[16,6]{1,0:T(8,128)S(1)} %get-tuple-element.359) | copy-start | bytes 1156 | tf_op jit(solution)/shard_map/while
  233.1 7.2 %copy-start.3 = (bf16[22,192,256]{2,1,0:T(8,128)(2,1)}, bf16[22,192,256]{2,1,0:T(8,128)(2,1)S(1)}, u32[]{:S(2)}) copy-start(bf16[22,192,256]{2,1,0:T(8,128)(2,1)S(1)} %get-tuple-element.358) | copy-start | bytes 6488068 | tf_op jit(solution)/shard_map/while
  233.1 7.2 %copy-start.9 = (s32[16,6]{1,0:T(8,128)}, s32[16,6]{1,0:T(8,128)S(1)}, u32[]{:S(2)}) copy-start(s32[16,6]{1,0:T(8,128)S(1)} %get-tuple-element.359) | copy-start | bytes 1156 | tf_op jit(solution)/shard_map/while
  261.9 7.2 %copy-start.3 = (bf16[22,192,256]{2,1,0:T(8,128)(2,1)}, bf16[22,192,256]{2,1,0:T(8,128)(2,1)S(1)}, u32[]{:S(2)}) copy-start(bf16[22,192,256]{2,1,0:T(8,128)(2,1)S(1)} %get-tuple-element.358) | copy-start | bytes 6488068 | tf_op jit(solution)/shard_map/while
  261.9 7.2 %copy-start.9 = (s32[16,6]{1,0:T(8,128)}, s32[16,6]{1,0:T(8,128)S(1)}, u32[]{:S(2)}) copy-start(s32[16,6]{1,0:T(8,128)S(1)} %get-tuple-element.359) | copy-start | bytes 1156 | tf_op jit(solution)/shard_map/while
  319.7 7.2 %copy-start.9 = (s32[16,6]{1,0:T(8,128)}, s32[16,6]{1,0:T(8,128)S(1)}, u32[]{:S(2)}) copy-start(s32[16,6]{1,0:T(8,128)S(1)} %get-tuple-element.359) | copy-start | bytes 1156 | tf_op jit(solution)/shard_map/while
  435.1 7.2 %copy-start.3 = (bf16[22,192,256]{2,1,0:T(8,128)(2,1)}, bf16[22,192,256]{2,1,0:T(8,128)(2,1)S(1)}, u32[]{:S(2)}) copy-start(bf16[22,192,256]{2,1,0:T(8,128)(2,1)S(1)} %get-tuple-element.358) | copy-start | bytes 6488068 | tf_op jit(solution)/shard_map/while
  435.1 7.2 %copy-start.9 = (s32[16,6]{1,0:T(8,128)}, s32[16,6]{1,0:T(8,128)S(1)}, u32[]{:S(2)}) copy-start(s32[16,6]{1,0:T(8,128)S(1)} %get-tuple-element.359) | copy-start | bytes 1156 | tf_op jit(solution)/shard_map/while
  463.9 7.2 %copy-start.3 = (bf16[22,192,256]{2,1,0:T(8,128)(2,1)}, bf16[22,192,256]{2,1,0:T(8,128)(2,1)S(1)}, u32[]{:S(2)}) copy-start(bf16[22,192,256]{2,1,0:T(8,128)(2,1)S(1)} %get-tuple-element.358) | copy-start | bytes 6488068 | tf_op jit(solution)/shard_map/while
  463.9 7.2 %copy-start.9 = (s32[16,6]{1,0:T(8,128)}, s32[16,6]{1,0:T(8,128)S(1)}, u32[]{:S(2)}) copy-start(s32[16,6]{1,0:T(8,128)S(1)} %get-tuple-element.359) | copy-start | bytes 1156 | tf_op jit(solution)/shard_map/while
  510.0 16.8 %collective-permute-start.2 = (bf16[16,64,256]{2,1,0:T(8,128)(2,1)S(1)}, bf16[16,64,256]{2,1,0:T(8,128)(2,1)S(1)}, u32[]{:S(2)}, u32[]{:S(2)}) collective-permute-start(bf16[16,64,256]{2,1,0:T(8,128)(2,1)S(1)} %get-tuple-element.273), channel_id=1, source_target_pairs={{0,1},{1,2},{2,3},{3,4},{4,5},{5,6},{6,7},{7,8},{8,9},{9,10},{10,1... | collective-permute-start | bytes 1572872 | tf_op jit(solution)/shard_map/ppermute | solution.py:26
  513.8 15.7 %collective-permute-start.3 = (bf16[16,64,256]{2,1,0:T(8,128)(2,1)S(1)}, bf16[16,64,256]{2,1,0:T(8,128)(2,1)S(1)}, u32[]{:S(2)}, u32[]{:S(2)}) collective-permute-start(bf16[16,64,256]{2,1,0:T(8,128)(2,1)S(1)} %get-tuple-element.274), channel_id=1, source_target_pairs={{0,15},{1,0},{2,1},{3,2},{4,3},{5,4},{6,5},{7,6},{8,7},{9,8},{10,9... | collective-permute-start | bytes 1572872 | tf_op jit(solution)/shard_map/ppermute | solution.py:26
  (100 other events, 362.2 us)
Sparse Core Ops, SparseCore 0:
  507.3 101.4 all-reduce.2
where the time goes:
time: 629 us; the launch traced here: 619 us
  local copies, waits for them, and re-layouts  378 us (60%)
  matrix products  118 us (19%)
  waiting for transfers between devices  90.4 us (14%)
  between operations  14.1 us (2%)
  other arithmetic  12.7 us (2%)
    reshape x16, local copies, waits for them, and re-layouts, banded(): return repeated.reshape(filters, blocks, rows_a, span - 1)[:, :, :, :cols_c]  111 us
    another operation x32, local copies, waits for them, and re-layouts, banded(): repeated = jnp.tile(profile, (1, 1, rows_a))[:, :, :rows_a * (span - 1)]  96.4 us
    psum x1, waiting for transfers between devices, shards(): summed = lax.psum(local_grad, 'lon')  76.9 us
    dynamic_slice x16, local copies, waits for them, and re-layouts, step_row(): lax.dynamic_slice(total, (i, 0, 0), (stack_rows, padded_width, channels))  40.7 us
    dot_general x16, matrix products, step_row(): jnp.einsum('bd,bwc->dwc', selector.astype(jnp.float32), pieces, precision...  34.8 us
    squeeze x16, local copies, waits for them, and re-layouts, step_row(): grad_row = lax.dynamic_index_in_dim(grad_basis, i, 0, keepdims=False)  30 us
    slice x16, local copies, waits for them, and re-layouts, banded(): repeated = jnp.tile(profile, (1, 1, rows_a))[:, :, :rows_a * (span - 1)]  25 us
    dynamic_update_slice x16, local copies, waits for them, and re-layouts, step_row(): total = lax.dynamic_update_slice(total, current + spread, (i, 0, 0))  24.2 us
  transfers between devices with their start and end apart: 5, of which 3 were waited for; matrix products, arithmetic and copies ran while one was open for 4% of the time, Pallas kernels for 0%

commit v1 on v0

v1 whole, which is shorter than its diff:
```python
import math

import jax
import jax.numpy as jnp
from jax import lax
from jax.experimental import pallas as pl
from jax.experimental.pallas import tpu as pltpu
from jax.sharding import PartitionSpec as P

VM = pl.BlockSpec(memory_space=pltpu.VMEM)
SM = pl.BlockSpec(memory_space=pltpu.SMEM)


def build_band(i, counts, quad, band, filters, blocks, cols):
    for b in range(blocks):
        live = (b < counts[i]).astype(jnp.float32)
        for k in range(filters):
            row = quad[k, i, pl.ds(b, 1), :] * live
            wide = jnp.broadcast_to(row, (cols, row.shape[1]))
            wide = pltpu.roll(wide, 0, 1, stride=1, stride_axis=0)
            band[k * cols : (k + 1) * cols, b * 128 : (b + 1) * 128] = wide.astype(jnp.bfloat16)


def forward_kernel(counts, rows, offs, before, source, after, quad, weight, cot, mixed, grad, ext, band, picked, basis):
    lat, cols, ch = source.shape
    filters = quad.shape[0]
    blocks = rows.shape[1]
    reach = before.shape[1]
    ext[:, :reach, :] = before[...].astype(jnp.float32)
    ext[:, reach : reach + cols, :] = source[...].astype(jnp.float32)
    ext[:, reach + cols : 2 * reach + cols, :] = after[...].astype(jnp.float32)

    def step(i, _):
        build_band(i, counts, quad, band, filters, blocks, cols)
        for b in range(blocks):
            start = offs[i, b] + reach
            shift = start % 8
            near = ext[rows[i, b], pl.ds(pl.multiple_of(start - shift, 8), 136), :].reshape(17, 8, ch)
            near = pltpu.roll(near, (8 - shift) % 8, 1)
            place = lax.broadcasted_iota(jnp.int32, (16, 8, ch), 1)
            near = jnp.where(place < 8 - shift, near[:16], near[1:]).reshape(128, ch)
            picked[b * 128 : (b + 1) * 128, :] = near.astype(jnp.bfloat16)
        here = pl.ds(pl.multiple_of(i * cols, cols), cols)
        out = jnp.dot(band[...], picked[...], preferred_element_type=jnp.float32).astype(jnp.bfloat16)
        for k in range(filters):
            basis[here, k * ch : (k + 1) * ch] = out[k * cols : (k + 1) * cols]
        return 0

    lax.fori_loop(0, lat, step, 0)
    total = lat * cols
    tile = 256

    def mix(m, _):
        here = pl.ds(pl.multiple_of(m * tile, tile), tile)
        mixed[here, :] = jnp.dot(basis[here, :], weight[...], preferred_element_type=jnp.float32).astype(jnp.bfloat16)
        return 0

    lax.fori_loop(0, total // tile, mix, 0)
    for k in range(filters):
        here = slice(k * ch, (k + 1) * ch)
        grad[here, :] = lax.dot_general(
            basis[:, here], cot[...], (((0,), (0,)), ((), ())), preferred_element_type=jnp.float32
        )


def backward_kernel(counts, rows, offs, quad, weight, cot, inner, west, east, total, band, grads):
    lat, cols, ch = inner.shape
    filters = quad.shape[0]
    blocks = rows.shape[1]
    reach = west.shape[1]
    total[...] = jnp.zeros_like(total)
    for k in range(filters):
        part = lax.dot_general(
            cot[...],
            weight[k * ch : (k + 1) * ch, :],
            (((1,), (1,)), ((), ())),
            preferred_element_type=jnp.float32,
        ).astype(jnp.bfloat16)
        grads[:, k * cols : (k + 1) * cols, :] = part.reshape(lat, cols, ch)

    def step(i, _):
        build_band(i, counts, quad, band, filters, blocks, cols)
        parts = lax.dot_general(
            band[...], grads[i], (((0,), (0,)), ((), ())), preferred_element_type=jnp.float32
        )
        for b in range(blocks):
            start = offs[i, b] + reach
            shift = start % 8
            far = pltpu.roll(parts[b * 128 : (b + 1) * 128].reshape(16, 8, ch), shift, 1)
            zero = jnp.zeros((1, 8, ch), jnp.float32)
            place = lax.broadcasted_iota(jnp.int32, (17, 8, ch), 1)
            far = jnp.where(
                place >= shift, jnp.concatenate([far, zero], axis=0), jnp.concatenate([zero, far], axis=0)
            )
            here = pl.ds(pl.multiple_of(start - shift, 8), 136)
            total[rows[i, b], here, :] += far.reshape(136, ch)
        return 0

    lax.fori_loop(0, lat, step, 0)
    west[...] = total[:, :reach, :].astype(jnp.bfloat16)
    inner[...] = total[:, reach : reach + cols, :]
    east[...] = total[:, reach + cols : 2 * reach + cols, :].astype(jnp.bfloat16)


def shards(source, quadrature, block_rows, offsets, counts, weight, cotangent):
    lat, cols, ch = source.shape
    filters = weight.shape[0]
    blocks = block_rows.shape[1]
    reach = quadrature.shape[3]
    peers = lax.axis_size("lon")
    up = [(i, (i + 1) % peers) for i in range(peers)]
    down = [(j, i) for i, j in up]
    before = lax.ppermute(source[:, cols - reach :], "lon", up)
    after = lax.ppermute(source[:, :reach], "lon", down)
    quad = jnp.pad(quadrature.astype(jnp.float32), ((0, 0), (0, 0), (0, 0), (0, 128 - reach)))
    flat_weight = weight.reshape(filters * ch, ch)
    flat_cot = cotangent.reshape(lat * cols, ch)
    params = pltpu.CompilerParams(vmem_limit_bytes=48 * 2**20)
    wide = cols + 2 * reach + 8
    mixed, local = pl.pallas_call(
        forward_kernel,
        out_shape=[
            jax.ShapeDtypeStruct((lat * cols, ch), jnp.bfloat16),
            jax.ShapeDtypeStruct((filters * ch, ch), jnp.float32),
        ],
        in_specs=[SM] * 3 + [VM] * 6,
        out_specs=[VM] * 2,
        scratch_shapes=[
            pltpu.VMEM((lat, wide, ch), jnp.float32),
            pltpu.VMEM((filters * cols, blocks * 128), jnp.bfloat16),
            pltpu.VMEM((blocks * 128, ch), jnp.bfloat16),
            pltpu.VMEM((lat * cols, filters * ch), jnp.bfloat16),
        ],
        compiler_params=params,
        cost_estimate=pl.CostEstimate(flops=8_000_000_000, bytes_accessed=8_000_000, transcendentals=0),
        name="forward",
    )(counts, block_rows, offsets, before, source, after, quad, flat_weight, flat_cot)
    inner, west, east = pl.pallas_call(
        backward_kernel,
        out_shape=[
            jax.ShapeDtypeStruct((lat, cols, ch), jnp.float32),
            jax.ShapeDtypeStruct((lat, reach, ch), jnp.bfloat16),
            jax.ShapeDtypeStruct((lat, reach, ch), jnp.bfloat16),
        ],
        in_specs=[SM] * 3 + [VM] * 3,
        out_specs=[VM] * 3,
        scratch_shapes=[
            pltpu.VMEM((lat, wide, ch), jnp.float32),
            pltpu.VMEM((filters * cols, blocks * 128), jnp.bfloat16),
            pltpu.VMEM((lat, filters * cols, ch), jnp.bfloat16),
        ],
        compiler_params=params,
        cost_estimate=pl.CostEstimate(flops=8_000_000_000, bytes_accessed=8_000_000, transcendentals=0),
        name="backward",
    )(counts, block_rows, offsets, quad, flat_weight, flat_cot)
    summed = lax.psum(local, "lon")
    factor = 1.0 / math.sqrt(lat * cols * peers)
    grad_weight = (summed * factor).reshape(filters, ch, ch)
    west_in = lax.ppermute(east, "lon", up).astype(jnp.float32)
    east_in = lax.ppermute(west, "lon", down).astype(jnp.float32)
    inner = inner.at[:, :reach].add(west_in)
    grad_source = inner.at[:, cols - reach :].add(east_in)
    return (mixed.reshape(lat, cols, ch), grad_source, grad_weight)


def solution(mesh):
    return jax.shard_map(
        shards,
        mesh=mesh,
        in_specs=(P("groups", "lon", None), P(), P(), P(), P(), P(), P("groups", "lon", None)),
        out_specs=(P("groups", "lon", None), P("groups", "lon", None), P("groups", None, None)),
        check_vma=False,
    )
```

time: 629 us -> 155 us (0.25)
  the two profiles are of different devices: /device:TPU:29 before, /device:TPU:0 now
where the time goes in v1:
time: 155 us; the launch traced here: 154 us
  waiting for transfers between devices  86.5 us (56%)
  Pallas kernels  30.8 us (20%)
  between operations  14.1 us (9%)
  starting transfers between devices  10.5 us (7%)
  local copies, waits for them, and re-layouts  7.92 us (5%)
  other arithmetic  4.46 us (3%)
    psum x1, waiting for transfers between devices, shards(): summed = lax.psum(local, 'lon')  68.6 us
    pallas_call x1, Pallas kernels, shards(): pl.pallas_call(backward_kernel, out_shape=[jax.ShapeDtypeStruct((lat, col...  17 us
    pallas_call x1, Pallas kernels, shards(): pl.pallas_call(forward_kernel, out_shape=[jax.ShapeDtypeStruct((lat * col...  13.8 us
    ppermute x1, waiting for transfers between devices, shards(): west_in = lax.ppermute(east, 'lon', up).astype(jnp.float32)  13.3 us
    unnamed x17, local copies, waits for them, and re-layouts  7.92 us
    ppermute x1, starting transfers between devices, shards(): after = lax.ppermute(source[:, :reach], 'lon', down)  5.06 us
    ppermute x1, starting transfers between devices, shards(): west_in = lax.ppermute(east, 'lon', up).astype(jnp.float32)  4.93 us
    ppermute x1, waiting for transfers between devices, shards(): before = lax.ppermute(source[:, cols - reach:], 'lon', up)  4.51 us
  transfers between devices with their start and end apart: 5, of which 3 were waited for; matrix products, arithmetic and copies ran while one was open for 2% of the time, Pallas kernels for 11%

profile of v1, /device:TPU:0, one launch (start us, length us, event | category | flops | bytes accessed | tf_op | source)
XLA Modules:
  0.0 154.2 jit_solution(1291464239667117784)
XLA Ops:
  7.2 0.0 all-reduce.3.cloned.1.call-start
  7.2 0.5 collective-permute-start
  7.7 5.1 %collective-permute-start.1 = (bf16[16,64,256]{2,1,0:T(8,128)(2,1)}, bf16[16,64,256]{2,1,0:T(8,128)(2,1)S(1)}, u32[]{:S(2)}, u32[]{:S(2)}) collective-permute-start(bf16[16,64,256]{2,1,0:T(8,128)(2,1)} %source.1), channel_id=1, source_target_pairs={{1,0},{2,1},{3,2},{4,3},{5,4},{6,5},{7,6},{8,7},{9,8},{10,9},{11,1... | collective-permute-start | bytes 1572872 | tf_op jit(solution)/shard_map/ppermute | solution.py:114
  12.8 0.8 copy.11.rows
  13.5 0.8 copy.12.offs
  14.3 1.0 copy.10
  15.3 0.1 pad_convert_fusion.quad
  15.4 4.5 %collective-permute-done.before = bf16[16,64,256]{2,1,0:T(8,128)(2,1)S(1)} collective-permute-done((bf16[16,64,256]{2,1,0:T(8,128)(2,1)}, bf16[16,64,256]{2,1,0:T(8,128)(2,1)S(1)}, u32[]{:S(2)}, u32[]{:S(2)}) %collective-permute-start) | collective-permute-done | bytes 524320 | tf_op jit(solution)/shard_map/ppermute | solution.py:113
  19.9 0.0 collective-permute-done.1.after
  19.9 1.3 copy-done
  21.2 1.0 copy-done.2
  22.2 1.0 copy-done.3
  23.3 0.7 copy-done.5
  23.9 13.8 %forward.1 = (bf16[1024,256]{1,0:T(8,128)(2,1)}, f32[2304,256]{1,0:T(8,128)}) custom-call(s32[16]{0:T(128)S(1)} %copy-done.5, s32[16,6]{1,0:T(8,128)S(1)} %copy.11.rows, s32[16,6]{1,0:T(8,128)S(1)} %copy.12.offs, bf16[16,64,256]{2,1,0:T(8,128)(2,1)S(1)} %collective-permute-done.before, bf16[16,64,256]{2,1,0:T(8,128)(2,1)S(1)} %copy-done.2, ...), custom_call_target="tpu_custom_call" | custom-call | flops 8000000000 | bytes 8000000 | tf_op jit(solution)/shard_map/forward/pallas_call | solution.py:120
  37.7 0.0 all-reduce.3.cloned.1.call-update
  37.7 1.2 copy-done.1
  38.9 0.1 copy-done.4
  39.1 17.0 %backward.1 = (f32[16,64,256]{2,1,0:T(8,128)S(1)}, bf16[16,64,256]{2,1,0:T(8,128)(2,1)S(1)}, bf16[16,64,256]{2,1,0:T(8,128)(2,1)S(1)}) custom-call(s32[16]{0:T(128)S(1)} %copy-done.6, s32[16,6]{1,0:T(8,128)S(1)} %copy.11.rows, s32[16,6]{1,0:T(8,128)S(1)} %copy.12.offs, f32[9,16,6,128]{3,2,1,0:T(8,128)S(1)} %pad_convert_fusion.quad, ...), custom_call_target="tpu_custom_call" | custom-call | flops 8000000000 | bytes 8000000 | tf_op jit(solution)/shard_map/backward/pallas_call | solution.py:138
  56.1 4.9 %collective-permute-start.2 = (bf16[16,64,256]{2,1,0:T(8,128)(2,1)S(1)}, bf16[16,64,256]{2,1,0:T(8,128)(2,1)S(1)}, u32[]{:S(2)}, u32[]{:S(2)}) collective-permute-start(bf16[16,64,256]{2,1,0:T(8,128)(2,1)S(1)} %get-tuple-element.50), channel_id=1, source_target_pairs={{0,1},{1,2},{2,3},{3,4},{4,5},{5,6},{6,7},{7,8},{8,9},{9,10},{10,1... | collective-permute-start | bytes 1572872 | tf_op jit(solution)/shard_map/ppermute | solution.py:159
  61.0 0.0 collective-permute-start.3
  61.1 13.3 %collective-permute-done.2 = bf16[16,64,256]{2,1,0:T(8,128)(2,1)S(1)} collective-permute-done((bf16[16,64,256]{2,1,0:T(8,128)(2,1)S(1)}, bf16[16,64,256]{2,1,0:T(8,128)(2,1)S(1)}, u32[]{:S(2)}, u32[]{:S(2)}) %collective-permute-start.2) | collective-permute-done | bytes 524320 | tf_op jit(solution)/shard_map/ppermute | solution.py:159
  74.4 1.2 convert_add_fusion
  75.6 68.6 %all-reduce.3.cloned.1.call-done = f32[2304,256]{1,0:T(8,128)} async-done(((f32[2304,256]{1,0:T(8,128)}), f32[2304,256]{1,0:T(8,128)}) %all-reduce.3.cloned.1.call-update) | async-done | bytes 2359312 | tf_op jit(solution)/shard_map/psum | solution.py:156
  144.2 3.2 %broadcast_multiply_fusion = f32[2304,256]{1,0:T(8,128)} fusion(f32[2304,256]{1,0:T(8,128)} %all-reduce.3.cloned.1.call-done), kind=kLoop, calls=%fused_computation | loop fusion | flops 589824 | bytes 4718592 | tf_op jit(solution)/shard_map/mul | solution.py:158
  (9 shorter events, 0.0 us)
Async XLA Ops:
  7.2 137.0 %all-reduce.3.cloned.1.call-start = ((), (), s32[]{:S(2)}) async-start(), calls=%async_computation | async-start | bytes 4718592 | tf_op jit(solution)/shard_map/psum | solution.py:156
  7.2 12.7 %collective-permute-start = (bf16[16,64,256]{2,1,0:T(8,128)(2,1)}, bf16[16,64,256]{2,1,0:T(8,128)(2,1)S(1)}, u32[]{:S(2)}, u32[]{:S(2)}) collective-permute-start(bf16[16,64,256]{2,1,0:T(8,128)(2,1)} %source.1), channel_id=1, source_target_pairs={{0,1},{1,2},{2,3},{3,4},{4,5},{5,6},{6,7},{7,8},{8,9},{9,10},{10,1... | collective-permute-start | bytes 1572872 | tf_op jit(solution)/shard_map/ppermute | solution.py:113
  7.7 12.2 %collective-permute-start.1 = (bf16[16,64,256]{2,1,0:T(8,128)(2,1)}, bf16[16,64,256]{2,1,0:T(8,128)(2,1)S(1)}, u32[]{:S(2)}, u32[]{:S(2)}) collective-permute-start(bf16[16,64,256]{2,1,0:T(8,128)(2,1)} %source.1), channel_id=1, source_target_pairs={{1,0},{2,1},{3,2},{4,3},{5,4},{6,5},{7,6},{8,7},{9,8},{10,9},{11,1... | collective-permute-start | bytes 1572872 | tf_op jit(solution)/shard_map/ppermute | solution.py:114
  19.9 1.3 copy-start
  21.2 1.0 copy-start.2
  22.2 1.0 copy-start.3
  23.3 0.7 copy-start.5
  37.7 1.3 copy-start.1
  37.7 1.4 copy-start.4
  37.7 1.4 copy-start.6
  56.1 18.3 %collective-permute-start.2 = (bf16[16,64,256]{2,1,0:T(8,128)(2,1)S(1)}, bf16[16,64,256]{2,1,0:T(8,128)(2,1)S(1)}, u32[]{:S(2)}, u32[]{:S(2)}) collective-permute-start(bf16[16,64,256]{2,1,0:T(8,128)(2,1)S(1)} %get-tuple-element.50), channel_id=1, source_target_pairs={{0,1},{1,2},{2,3},{3,4},{4,5},{5,6},{6,7},{7,8},{8,9},{9,10},{10,1... | collective-permute-start | bytes 1572872 | tf_op jit(solution)/shard_map/ppermute | solution.py:159
  61.0 13.3 %collective-permute-start.3 = (bf16[16,64,256]{2,1,0:T(8,128)(2,1)S(1)}, bf16[16,64,256]{2,1,0:T(8,128)(2,1)S(1)}, u32[]{:S(2)}, u32[]{:S(2)}) collective-permute-start(bf16[16,64,256]{2,1,0:T(8,128)(2,1)S(1)} %get-tuple-element.51), channel_id=1, source_target_pairs={{1,0},{2,1},{3,2},{4,3},{5,4},{6,5},{7,6},{8,7},{9,8},{10,9},{11,1... | collective-permute-start | bytes 1572872 | tf_op jit(solution)/shard_map/ppermute | solution.py:160
Sparse Core Ops, SparseCore 0:
  37.8 106.2 all-reduce.2

commit v2 on v1

--- a/solution.py
+++ b/solution.py
@@ -8,6 +8,7 @@
 from jax.sharding import PartitionSpec as P
 
 VM = pl.BlockSpec(memory_space=pltpu.VMEM)
+MESH = pl.DeviceIdType.MESH
 SM = pl.BlockSpec(memory_space=pltpu.SMEM)
 
 
@@ -60,7 +61,9 @@
         here = slice(k * ch, (k + 1) * ch)
         grad[here, :] = lax.dot_general(
             basis[:, here], cot[...], (((0,), (0,)), ((), ())), preferred_element_type=jnp.float32
-        )
+        ).astype(jnp.bfloat16)
+    if grad.shape[0] > filters * ch:
+        grad[filters * ch :, :] = jnp.zeros((grad.shape[0] - filters * ch, ch), jnp.bfloat16)
 
 
 def backward_kernel(counts, rows, offs, quad, weight, cot, inner, west, east, total, band, grads):
@@ -102,6 +105,61 @@
     east[...] = total[:, reach + cols : 2 * reach + cols, :].astype(jnp.bfloat16)
 
 
+def sum_kernel(mine, out, paired, partial, others, sems):
+    groups, rows, ch = partial.shape
+    me = lax.axis_index("lon")
+    core = lax.rem(me, 2)
+    chip = lax.div(me, 2)
+    sibling = chip * 2 + 1 - core
+    peer = [lax.rem(chip + d, groups) * 2 + core for d in range(groups)]
+    barrier = pltpu.get_barrier_semaphore()
+    for other in [sibling] + peer[1:]:
+        pl.semaphore_signal(barrier, inc=1, device_id={"lon": other}, device_id_type=MESH)
+    pl.semaphore_wait(barrier, groups)
+
+    def copy(src, dst, phase, slot, other):
+        return pltpu.make_async_remote_copy(
+            src_ref=src,
+            dst_ref=dst,
+            send_sem=sems.at[phase, 0, slot],
+            recv_sem=sems.at[phase, 1, slot],
+            device_id={"lon": other},
+            device_id_type=MESH,
+        )
+
+    pairs = []
+    for d in list(range(1, groups)) + [0]:
+        q = lax.rem(chip + d, groups)
+        pairs.append((d, q, copy(mine.at[1 - core, q], paired.at[d], 0, d, sibling)))
+        pairs[-1][2].start()
+    crossing = []
+    for d, q, pair in pairs:
+        pair.wait()
+        both = mine[core, q].astype(jnp.float32) + paired[d].astype(jnp.float32)
+        partial[d] = both.astype(jnp.bfloat16)
+        if d > 0:
+            crossing.append(copy(partial.at[d], others.at[d], 1, d, peer[d]))
+            crossing[-1].start()
+    total = partial[0].astype(jnp.float32)
+    for d in range(1, groups):
+        crossing[d - 1].wait()
+        total = total + others[d].astype(jnp.float32)
+    out[core, chip] = total.astype(jnp.bfloat16)
+    spread = []
+    for d in range(1, groups):
+        spread.append(copy(out.at[core, chip], out.at[core, chip], 2, d, peer[d]))
+        spread[-1].start()
+    handed = [copy(out.at[core, chip], out.at[core, chip], 3, 0, sibling)]
+    handed[0].start()
+    for d in range(1, groups):
+        spread[d - 1].wait()
+        came = lax.rem(chip - d + groups, groups)
+        handed.append(copy(out.at[core, came], out.at[core, came], 3, d, sibling))
+        handed[-1].start()
+    for one in handed:
+        one.wait()
+
+
 def shards(source, quadrature, block_rows, offsets, counts, weight, cotangent):
     lat, cols, ch = source.shape
     filters = weight.shape[0]
@@ -116,12 +174,13 @@
     flat_weight = weight.reshape(filters * ch, ch)
     flat_cot = cotangent.reshape(lat * cols, ch)
     params = pltpu.CompilerParams(vmem_limit_bytes=48 * 2**20)
+    chunk = -(-filters * ch // (16 * peers)) * 16
     wide = cols + 2 * reach + 8
     mixed, local = pl.pallas_call(
         forward_kernel,
         out_shape=[
             jax.ShapeDtypeStruct((lat * cols, ch), jnp.bfloat16),
-            jax.ShapeDtypeStruct((filters * ch, ch), jnp.float32),
+            jax.ShapeDtypeStruct((peers * chunk, ch), jnp.bfloat16),
         ],
         in_specs=[SM] * 3 + [VM] * 6,
         out_specs=[VM] * 2,
@@ -153,7 +212,21 @@
         cost_estimate=pl.CostEstimate(flops=8_000_000_000, bytes_accessed=8_000_000, transcendentals=0),
         name="backward",
     )(counts, block_rows, offsets, quad, flat_weight, flat_cot)
-    summed = lax.psum(local, "lon")
+    groups = peers // 2
+    summed = pl.pallas_call(
+        sum_kernel,
+        out_shape=jax.ShapeDtypeStruct((2, groups, chunk, ch), jnp.bfloat16),
+        in_specs=[VM],
+        out_specs=VM,
+        scratch_shapes=[pltpu.VMEM((groups, chunk, ch), jnp.bfloat16)] * 3
+        + [pltpu.SemaphoreType.DMA((4, 2, groups))],
+        compiler_params=pltpu.CompilerParams(
+            vmem_limit_bytes=32 * 2**20, collective_id=0, has_side_effects=True
+        ),
+        cost_estimate=pl.CostEstimate(flops=30_000_000_000, bytes_accessed=60_000_000, transcendentals=0),
+        name="weight_sum",
+    )(local.reshape(2, groups, chunk, ch))
+    summed = summed.reshape(peers * chunk, ch)[: filters * ch].astype(jnp.float32)
     factor = 1.0 / math.sqrt(lat * cols * peers)
     grad_weight = (summed * factor).reshape(filters, ch, ch)
     west_in = lax.ppermute(east, "lon", up).astype(jnp.float32)

time: 155 us -> 79.5 us (0.51)
  the two profiles are of different devices: /device:TPU:0 before, /device:TPU:29 now
where the time goes in v2:
time: 79.5 us; the launch traced here: 79.2 us
  Pallas kernels  64.8 us (82%)
  local copies, waits for them, and re-layouts  5.51 us (7%)
  starting transfers between devices  5.28 us (7%)
  other arithmetic  2.88 us (4%)
    pallas_call x1, Pallas kernels, shards(): pl.pallas_call(sum_kernel, out_shape=jax.ShapeDtypeStruct((2, groups, chu...  34.8 us
    pallas_call x1, Pallas kernels, shards(): pl.pallas_call(backward_kernel, out_shape=[jax.ShapeDtypeStruct((lat, col...  17 us
    pallas_call x1, Pallas kernels, shards(): pl.pallas_call(forward_kernel, out_shape=[jax.ShapeDtypeStruct((lat * col...  13 us
    unnamed x13, local copies, waits for them, and re-layouts  5.51 us
    ppermute x1, starting transfers between devices, shards(): west_in = lax.ppermute(east, 'lon', up).astype(jnp.float32)  2.77 us
    ppermute x1, starting transfers between devices, shards(): east_in = lax.ppermute(west, 'lon', down).astype(jnp.float32)  1.73 us
    mul x1, other arithmetic, shards(): grad_weight = (summed * factor).reshape(filters, ch, ch)  1.65 us
  transfers between devices with their start and end apart: 4, of which 0 were waited for; matrix products, arithmetic and copies ran while one was open for 5% of the time, Pallas kernels for 82%

profile of v2, /device:TPU:29, one launch (start us, length us, event | category | flops | bytes accessed | tf_op | source)
XLA Modules:
  0.0 79.2 jit_solution(128722240085285152)
XLA Ops:
  0.6 0.1 collective-permute-start
  0.7 0.7 collective-permute-start.1
  1.4 0.8 copy.11.rows
  2.2 0.8 copy.12.offs
  3.0 1.0 %copy.10 = bf16[9,16,6,64]{3,2,1,0:T(8,128)(2,1)S(1)} copy(bf16[9,16,6,64]{3,1,2,0:T(8,128)(2,1)} %param.16) | data formatting | bytes 221184 | tf_op args[1]
  4.0 0.1 pad_convert_fusion.quad
  4.0 0.0 copy-start
  4.0 1.3 %copy-done = bf16[9,256,256]{2,1,0:T(8,128)(2,1)S(1)} copy-done((bf16[9,256,256]{2,1,0:T(8,128)(2,1)S(1)}, bf16[9,256,256]{2,1,0:T(8,128)(2,1)}, u32[]{:S(2)}) %copy-start) | copy-done | bytes 1179672
  5.3 0.0 copy-start.3
  5.3 1.0 %copy-done.3 = bf16[16,64,256]{2,1,0:T(8,128)(2,1)S(1)} copy-done((bf16[16,64,256]{2,1,0:T(8,128)(2,1)S(1)}, bf16[16,64,256]{2,1,0:T(8,128)(2,1)}, u32[]{:S(2)}) %copy-start.3) | copy-done | bytes 524312
  6.4 0.7 copy-done.4
  7.0 17.0 %backward.1 = (f32[16,64,256]{2,1,0:T(8,128)S(1)}, bf16[16,64,256]{2,1,0:T(8,128)(2,1)S(1)}, bf16[16,64,256]{2,1,0:T(8,128)(2,1)S(1)}) custom-call(s32[16]{0:T(128)S(1)} %copy-done.4, s32[16,6]{1,0:T(8,128)S(1)} %copy.11.rows, s32[16,6]{1,0:T(8,128)S(1)} %copy.12.offs, f32[9,16,6,128]{3,2,1,0:T(8,128)S(1)} %pad_convert_fusion.quad, ...), custom_call_target="tpu_custom_call" | custom-call | flops 8000000000 | bytes 8000000 | tf_op jit(solution)/shard_map/backward/pallas_call | solution.py:197
  24.0 1.7 %collective-permute-start.3 = (bf16[16,64,256]{2,1,0:T(8,128)(2,1)S(1)}, bf16[16,64,256]{2,1,0:T(8,128)(2,1)S(1)}, u32[]{:S(2)}, u32[]{:S(2)}) collective-permute-start(bf16[16,64,256]{2,1,0:T(8,128)(2,1)S(1)} %get-tuple-element.51), channel_id=1, source_target_pairs={{1,0},{2,1},{3,2},{4,3},{5,4},{6,5},{7,6},{8,7},{9,8},{10,9},{11,1... | collective-permute-start | bytes 1572872 | tf_op jit(solution)/shard_map/ppermute | solution.py:233
  25.8 2.8 %collective-permute-start.2 = (bf16[16,64,256]{2,1,0:T(8,128)(2,1)S(1)}, bf16[16,64,256]{2,1,0:T(8,128)(2,1)S(1)}, u32[]{:S(2)}, u32[]{:S(2)}) collective-permute-start(bf16[16,64,256]{2,1,0:T(8,128)(2,1)S(1)} %get-tuple-element.50), channel_id=1, source_target_pairs={{0,1},{1,2},{2,3},{3,4},{4,5},{5,6},{6,7},{7,8},{8,9},{9,10},{10,1... | collective-permute-start | bytes 1572872 | tf_op jit(solution)/shard_map/ppermute | solution.py:232
  28.5 0.0 collective-permute-done.before
  28.5 0.0 collective-permute-done.1.after
  28.5 0.0 copy-done.1
  28.6 0.0 copy-done.2
  28.6 13.0 %forward.1 = (bf16[1024,256]{1,0:T(8,128)(2,1)}, bf16[2304,256]{1,0:T(8,128)(2,1)S(1)}) custom-call(s32[16]{0:T(128)S(1)} %copy-done.4, s32[16,6]{1,0:T(8,128)S(1)} %copy.11.rows, s32[16,6]{1,0:T(8,128)S(1)} %copy.12.offs, bf16[16,64,256]{2,1,0:T(8,128)(2,1)S(1)} %collective-permute-done.before, bf16[16,64,256]{2,1,0:T(8,128)(2,1)S(1)} %copy-done.2, ...), custom_call_target="tpu_custom_call" | custom-call | flops 8000000000 | bytes 8000000 | tf_op jit(solution)/shard_map/forward/pallas_call | solution.py:179
  41.5 34.8 %weight_sum.1 = bf16[2,8,144,256]{3,2,1,0:T(8,128)(2,1)S(1)} custom-call(bf16[2,8,144,256]{3,2,1,0:T(8,128)(2,1)S(1)} %bitcast.9), custom_call_target="tpu_custom_call" | custom-call | flops 30000001024 | bytes 60000000 | tf_op jit(solution)/shard_map/weight_sum/pallas_call | solution.py:216
  76.4 1.6 %convert_multiply_fusion = f32[2,8,144,256]{3,2,1,0:T(8,128)} fusion(bf16[2,8,144,256]{3,2,1,0:T(8,128)(2,1)S(1)} %weight_sum.1), kind=kLoop, calls=%fused_computation | loop fusion | flops 1179648 | bytes 3538944 | tf_op jit(solution)/shard_map/mul | solution.py:231
  78.0 0.0 collective-permute-done.3
  78.0 0.0 collective-permute-done.2
  78.0 1.2 %convert_add_fusion = f32[16,64,256]{2,1,0:T(8,128)} fusion(bf16[16,64,256]{2,1,0:T(8,128)(2,1)S(1)} %collective-permute-done.3, f32[16,64,256]{2,1,0:T(8,128)S(1)} %get-tuple-element.49, bf16[16,64,256]{2,1,0:T(8,128)(2,1)S(1)} %collective-permute-done.2), kind=kLoop, calls=%fused_computation.1 | loop fusion | flops 1048576 | bytes 3145728 | tf_op jit(solution)/shard_map/add | solution.py:235
  (3 shorter events, 0.0 us)
Async XLA Ops:
  0.6 27.9 %collective-permute-start = (bf16[16,64,256]{2,1,0:T(8,128)(2,1)}, bf16[16,64,256]{2,1,0:T(8,128)(2,1)S(1)}, u32[]{:S(2)}, u32[]{:S(2)}) collective-permute-start(bf16[16,64,256]{2,1,0:T(8,128)(2,1)} %source.1), channel_id=1, source_target_pairs={{0,1},{1,2},{2,3},{3,4},{4,5},{5,6},{6,7},{7,8},{8,9},{9,10},{10,1... | collective-permute-start | bytes 1572872 | tf_op jit(solution)/shard_map/ppermute | solution.py:171
  0.7 27.8 %collective-permute-start.1 = (bf16[16,64,256]{2,1,0:T(8,128)(2,1)}, bf16[16,64,256]{2,1,0:T(8,128)(2,1)S(1)}, u32[]{:S(2)}, u32[]{:S(2)}) collective-permute-start(bf16[16,64,256]{2,1,0:T(8,128)(2,1)} %source.1), channel_id=1, source_target_pairs={{1,0},{2,1},{3,2},{4,3},{5,4},{6,5},{7,6},{8,7},{9,8},{10,9},{11,1... | collective-permute-start | bytes 1572872 | tf_op jit(solution)/shard_map/ppermute | solution.py:172
  4.0 1.3 %copy-start = (bf16[9,256,256]{2,1,0:T(8,128)(2,1)S(1)}, bf16[9,256,256]{2,1,0:T(8,128)(2,1)}, u32[]{:S(2)}) copy-start(bf16[9,256,256]{2,1,0:T(8,128)(2,1)} %param.20) | copy-start | bytes 3538948
  5.3 1.0 %copy-start.3 = (bf16[16,64,256]{2,1,0:T(8,128)(2,1)S(1)}, bf16[16,64,256]{2,1,0:T(8,128)(2,1)}, u32[]{:S(2)}) copy-start(bf16[16,64,256]{2,1,0:T(8,128)(2,1)} %param.21) | copy-start | bytes 1572868
  6.4 0.7 copy-start.4
  7.0 21.5 %copy-start.1 = (bf16[9,256,256]{2,1,0:T(8,128)(2,1)S(1)}, bf16[9,256,256]{2,1,0:T(8,128)(2,1)}, u32[]{:S(2)}) copy-start(bf16[9,256,256]{2,1,0:T(8,128)(2,1)} %param.20) | copy-start | bytes 3538948
  7.0 21.5 %copy-start.2 = (bf16[16,64,256]{2,1,0:T(8,128)(2,1)S(1)}, bf16[16,64,256]{2,1,0:T(8,128)(2,1)}, u32[]{:S(2)}) copy-start(bf16[16,64,256]{2,1,0:T(8,128)(2,1)} %source.1) | copy-start | bytes 1572868
  24.0 54.0 %collective-permute-start.3 = (bf16[16,64,256]{2,1,0:T(8,128)(2,1)S(1)}, bf16[16,64,256]{2,1,0:T(8,128)(2,1)S(1)}, u32[]{:S(2)}, u32[]{:S(2)}) collective-permute-start(bf16[16,64,256]{2,1,0:T(8,128)(2,1)S(1)} %get-tuple-element.51), channel_id=1, source_target_pairs={{1,0},{2,1},{3,2},{4,3},{5,4},{6,5},{7,6},{8,7},{9,8},{10,9},{11,1... | collective-permute-start | bytes 1572872 | tf_op jit(solution)/shard_map/ppermute | solution.py:233
  25.8 52.2 %collective-permute-start.2 = (bf16[16,64,256]{2,1,0:T(8,128)(2,1)S(1)}, bf16[16,64,256]{2,1,0:T(8,128)(2,1)S(1)}, u32[]{:S(2)}, u32[]{:S(2)}) collective-permute-start(bf16[16,64,256]{2,1,0:T(8,128)(2,1)S(1)} %get-tuple-element.50), channel_id=1, source_target_pairs={{0,1},{1,2},{2,3},{3,4},{4,5},{5,6},{6,7},{7,8},{8,9},{9,10},{10,1... | collective-permute-start | bytes 1572872 | tf_op jit(solution)/shard_map/ppermute | solution.py:232

commit v3 on v1

--- a/solution.py
+++ b/solution.py
@@ -8,7 +8,13 @@
 from jax.sharding import PartitionSpec as P
 
 VM = pl.BlockSpec(memory_space=pltpu.VMEM)
+MESH = pl.DeviceIdType.MESH
 SM = pl.BlockSpec(memory_space=pltpu.SMEM)
+
+
+def by_count(count, blocks, run):
+    for n in range(2, blocks + 1, 2):
+        pl.when((count > n - 2) & (count <= n))(lambda n=n: run(n))
 
 
 def build_band(i, counts, quad, band, filters, blocks, cols):
@@ -30,7 +36,7 @@
     ext[:, reach : reach + cols, :] = source[...].astype(jnp.float32)
     ext[:, reach + cols : 2 * reach + cols, :] = after[...].astype(jnp.float32)
 
-    def step(i, _):
+    def live_step(i, blocks):
         build_band(i, counts, quad, band, filters, blocks, cols)
         for b in range(blocks):
             start = offs[i, b] + reach
@@ -41,9 +47,13 @@
             near = jnp.where(place < 8 - shift, near[:16], near[1:]).reshape(128, ch)
             picked[b * 128 : (b + 1) * 128, :] = near.astype(jnp.bfloat16)
         here = pl.ds(pl.multiple_of(i * cols, cols), cols)
-        out = jnp.dot(band[...], picked[...], preferred_element_type=jnp.float32).astype(jnp.bfloat16)
+        used = slice(0, blocks * 128)
+        out = jnp.dot(band[:, used], picked[used, :], preferred_element_type=jnp.float32).astype(jnp.bfloat16)
         for k in range(filters):
             basis[here, k * ch : (k + 1) * ch] = out[k * cols : (k + 1) * cols]
+
+    def step(i, _):
+        by_count(counts[i], blocks, lambda n: live_step(i, n))
         return 0
 
     lax.fori_loop(0, lat, step, 0)
@@ -60,7 +70,9 @@
         here = slice(k * ch, (k + 1) * ch)
         grad[here, :] = lax.dot_general(
             basis[:, here], cot[...], (((0,), (0,)), ((), ())), preferred_element_type=jnp.float32
-        )
+        ).astype(jnp.bfloat16)
+    if grad.shape[0] > filters * ch:
+        grad[filters * ch :, :] = jnp.zeros((grad.shape[0] - filters * ch, ch), jnp.bfloat16)
 
 
 def backward_kernel(counts, rows, offs, quad, weight, cot, inner, west, east, total, band, grads):
@@ -78,10 +90,10 @@
         ).astype(jnp.bfloat16)
         grads[:, k * cols : (k + 1) * cols, :] = part.reshape(lat, cols, ch)
 
-    def step(i, _):
+    def live_step(i, blocks):
         build_band(i, counts, quad, band, filters, blocks, cols)
         parts = lax.dot_general(
-            band[...], grads[i], (((0,), (0,)), ((), ())), preferred_element_type=jnp.float32
+            band[:, : blocks * 128], grads[i], (((0,), (0,)), ((), ())), preferred_element_type=jnp.float32
         )
         for b in range(blocks):
             start = offs[i, b] + reach
@@ -94,12 +106,91 @@
             )
             here = pl.ds(pl.multiple_of(start - shift, 8), 136)
             total[rows[i, b], here, :] += far.reshape(136, ch)
+
+    def step(i, _):
+        by_count(counts[i], blocks, lambda n: live_step(i, n))
         return 0
 
     lax.fori_loop(0, lat, step, 0)
     west[...] = total[:, :reach, :].astype(jnp.bfloat16)
     inner[...] = total[:, reach : reach + cols, :]
     east[...] = total[:, reach + cols : 2 * reach + cols, :].astype(jnp.bfloat16)
+
+
+def sum_kernel(mine, out, paired, half, level, partial, others, sems):
+    groups, rows, ch = partial.shape
+    me = lax.axis_index("lon")
+    core = lax.rem(me, 2)
+    side = lax.rem(lax.div(me, 2), 2)
+    ring = lax.div(me, 4)
+    sibling = me + 1 - 2 * core
+    across = me + 2 - 4 * side
+    spot = [lax.rem(ring + d, groups) for d in range(groups)]
+    peer = [spot[d] * 4 + side * 2 + core for d in range(groups)]
+    barrier = pltpu.get_barrier_semaphore()
+    for other in [sibling, across] + peer[1:]:
+        pl.semaphore_signal(barrier, inc=1, device_id={"lon": other}, device_id_type=MESH)
+    pl.semaphore_wait(barrier, groups + 1)
+
+    def send(src, dst, phase, slot, other):
+        copy = pltpu.make_async_remote_copy(
+            src_ref=src,
+            dst_ref=dst,
+            send_sem=sems.at[phase, 0, slot],
+            recv_sem=sems.at[phase, 1, slot],
+            device_id={"lon": other},
+            device_id_type=MESH,
+        )
+        copy.start()
+        return copy
+
+    order = list(range(1, groups)) + [0]
+    line = [side, 1 - side]
+    pairs = {}
+    for t in (1, 0):
+        for d in order:
+            pairs[t, d] = send(mine.at[1 - core, line[t], spot[d]], paired.at[t, d], 0, t * groups + d, sibling)
+
+    def both(t, d):
+        pairs[t, d].wait()
+        return mine[core, line[t], spot[d]].astype(jnp.float32) + paired[t, d].astype(jnp.float32)
+
+    sides = {}
+    for d in order:
+        half[d] = both(1, d).astype(jnp.bfloat16)
+        sides[d] = send(half.at[d], level.at[d], 1, d, across)
+    crossing = {}
+    for d in order:
+        own = both(0, d)
+        sides[d].wait()
+        own = own + level[d].astype(jnp.float32)
+        if d > 0:
+            partial[d] = own.astype(jnp.bfloat16)
+            crossing[d] = send(partial.at[d], others.at[d], 2, d, peer[d])
+    for d in range(1, groups):
+        crossing[d].wait()
+        own = own + others[d].astype(jnp.float32)
+    out[core, side, ring] = own.astype(jnp.bfloat16)
+
+    def share(c, slot, phase, place, other):
+        ref = out.at[core, c, place]
+        return send(ref, ref, phase, slot, other)
+
+    far = [share(side, d, 3, ring, peer[d]) for d in range(1, groups)]
+    near = []
+    last = []
+    for d in range(groups):
+        if d > 0:
+            far[d - 1].wait()
+        came = lax.rem(ring - d + groups, groups)
+        near.append(share(side, d, 4, came, across))
+        last.append(share(side, d, 5, came, sibling))
+    for d in range(groups):
+        near[d].wait()
+        came = lax.rem(ring - d + groups, groups)
+        last.append(share(1 - side, groups + d, 5, came, sibling))
+    for one in last:
+        one.wait()
 
 
 def shards(source, quadrature, block_rows, offsets, counts, weight, cotangent):
@@ -116,12 +207,13 @@
     flat_weight = weight.reshape(filters * ch, ch)
     flat_cot = cotangent.reshape(lat * cols, ch)
     params = pltpu.CompilerParams(vmem_limit_bytes=48 * 2**20)
+    chunk = -(-filters * ch // (16 * peers)) * 16
     wide = cols + 2 * reach + 8
     mixed, local = pl.pallas_call(
         forward_kernel,
         out_shape=[
             jax.ShapeDtypeStruct((lat * cols, ch), jnp.bfloat16),
-            jax.ShapeDtypeStruct((filters * ch, ch), jnp.float32),
+            jax.ShapeDtypeStruct((peers * chunk, ch), jnp.bfloat16),
         ],
         in_specs=[SM] * 3 + [VM] * 6,
         out_specs=[VM] * 2,
@@ -153,7 +245,22 @@
         cost_estimate=pl.CostEstimate(flops=8_000_000_000, bytes_accessed=8_000_000, transcendentals=0),
         name="backward",
     )(counts, block_rows, offsets, quad, flat_weight, flat_cot)
-    summed = lax.psum(local, "lon")
+    groups = peers // 4
+    summed = pl.pallas_call(
+        sum_kernel,
+        out_shape=jax.ShapeDtypeStruct((2, 2, groups, chunk, ch), jnp.bfloat16),
+        in_specs=[VM],
+        out_specs=VM,
+        scratch_shapes=[pltpu.VMEM((2, groups, chunk, ch), jnp.bfloat16)]
+        + [pltpu.VMEM((groups, chunk, ch), jnp.bfloat16)] * 4
+        + [pltpu.SemaphoreType.DMA((6, 2, 2 * groups))],
+        compiler_params=pltpu.CompilerParams(
+            vmem_limit_bytes=32 * 2**20, collective_id=0, has_side_effects=True
+        ),
+        cost_estimate=pl.CostEstimate(flops=30_000_000_000, bytes_accessed=60_000_000, transcendentals=0),
+        name="weight_sum",
+    )(local.reshape(2, 2, groups, chunk, ch))
+    summed = summed.reshape(peers * chunk, ch)[: filters * ch].astype(jnp.float32)
     factor = 1.0 / math.sqrt(lat * cols * peers)
     grad_weight = (summed * factor).reshape(filters, ch, ch)
     west_in = lax.ppermute(east, "lon", up).astype(jnp.float32)

time: 155 us -> 68.4 us (0.44)
  the two profiles are of different devices: /device:TPU:0 before, /device:TPU:29 now
where the time goes in v3:
time: 68.4 us; the launch traced here: 67.3 us
  Pallas kernels  52.9 us (77%)
  local copies, waits for them, and re-layouts  5.51 us (8%)
  starting transfers between devices  5.28 us (8%)
  other arithmetic  2.88 us (4%)
  between operations  0.69 us (1%)
    pallas_call x1, Pallas kernels, shards(): pl.pallas_call(sum_kernel, out_shape=jax.ShapeDtypeStruct((2, 2, groups,...  29.3 us
    pallas_call x1, Pallas kernels, shards(): pl.pallas_call(backward_kernel, out_shape=[jax.ShapeDtypeStruct((lat, col...  12.4 us
    pallas_call x1, Pallas kernels, shards(): pl.pallas_call(forward_kernel, out_shape=[jax.ShapeDtypeStruct((lat * col...  11.2 us
    unnamed x13, local copies, waits for them, and re-layouts  5.51 us
    ppermute x1, starting transfers between devices, shards(): west_in = lax.ppermute(east, 'lon', up).astype(jnp.float32)  2.76 us
    ppermute x1, starting transfers between devices, shards(): east_in = lax.ppermute(west, 'lon', down).astype(jnp.float32)  1.74 us
    mul x1, other arithmetic, shards(): grad_weight = (summed * factor).reshape(filters, ch, ch)  1.65 us
  transfers between devices with their start and end apart: 4, of which 0 were waited for; matrix products, arithmetic and copies ran while one was open for 6% of the time, Pallas kernels for 79%

profile of v3, /device:TPU:29, one launch (start us, length us, event | category | flops | bytes accessed | tf_op | source)
XLA Modules:
  0.0 67.3 jit_solution(16193732375153565443)
XLA Ops:
  0.6 0.1 collective-permute-start
  0.7 0.7 %collective-permute-start.1 = (bf16[16,64,256]{2,1,0:T(8,128)(2,1)}, bf16[16,64,256]{2,1,0:T(8,128)(2,1)S(1)}, u32[]{:S(2)}, u32[]{:S(2)}) collective-permute-start(bf16[16,64,256]{2,1,0:T(8,128)(2,1)} %source.1), channel_id=1, source_target_pairs={{1,0},{2,1},{3,2},{4,3},{5,4},{6,5},{7,6},{8,7},{9,8},{10,9},{11,1... | collective-permute-start | bytes 1572872 | tf_op jit(solution)/shard_map/ppermute | solution.py:205
  1.4 0.8 %copy.11.rows = s32[16,6]{1,0:T(8,128)S(1)} copy(s32[16,6]{0,1:T(8,128)} %param.17) | data formatting | bytes 768 | tf_op args[2]
  2.2 0.8 %copy.12.offs = s32[16,6]{1,0:T(8,128)S(1)} copy(s32[16,6]{0,1:T(8,128)} %param.18) | data formatting | bytes 768 | tf_op args[3]
  3.0 1.0 %copy.10 = bf16[9,16,6,64]{3,2,1,0:T(8,128)(2,1)S(1)} copy(bf16[9,16,6,64]{3,1,2,0:T(8,128)(2,1)} %param.16) | data formatting | bytes 221184 | tf_op args[1]
  4.0 0.1 pad_convert_fusion.quad
  4.0 0.0 copy-start
  4.0 1.3 %copy-done = bf16[9,256,256]{2,1,0:T(8,128)(2,1)S(1)} copy-done((bf16[9,256,256]{2,1,0:T(8,128)(2,1)S(1)}, bf16[9,256,256]{2,1,0:T(8,128)(2,1)}, u32[]{:S(2)}) %copy-start) | copy-done | bytes 1179672
  5.3 0.0 copy-start.3
  5.3 1.0 %copy-done.3 = bf16[16,64,256]{2,1,0:T(8,128)(2,1)S(1)} copy-done((bf16[16,64,256]{2,1,0:T(8,128)(2,1)S(1)}, bf16[16,64,256]{2,1,0:T(8,128)(2,1)}, u32[]{:S(2)}) %copy-start.3) | copy-done | bytes 524312
  6.4 0.7 copy-done.4
  7.0 12.4 %backward.1 = (f32[16,64,256]{2,1,0:T(8,128)S(1)}, bf16[16,64,256]{2,1,0:T(8,128)(2,1)S(1)}, bf16[16,64,256]{2,1,0:T(8,128)(2,1)S(1)}) custom-call(s32[16]{0:T(128)S(1)} %copy-done.4, s32[16,6]{1,0:T(8,128)S(1)} %copy.11.rows, s32[16,6]{1,0:T(8,128)S(1)} %copy.12.offs, f32[9,16,6,128]{3,2,1,0:T(8,128)S(1)} %pad_convert_fusion.quad, ...), custom_call_target="tpu_custom_call" | custom-call | flops 8000000000 | bytes 8000000 | tf_op jit(solution)/shard_map/backward/pallas_call | solution.py:230
  19.5 1.7 %collective-permute-start.3 = (bf16[16,64,256]{2,1,0:T(8,128)(2,1)S(1)}, bf16[16,64,256]{2,1,0:T(8,128)(2,1)S(1)}, u32[]{:S(2)}, u32[]{:S(2)}) collective-permute-start(bf16[16,64,256]{2,1,0:T(8,128)(2,1)S(1)} %get-tuple-element.51), channel_id=1, source_target_pairs={{1,0},{2,1},{3,2},{4,3},{5,4},{6,5},{7,6},{8,7},{9,8},{10,9},{11,1... | collective-permute-start | bytes 1572872 | tf_op jit(solution)/shard_map/ppermute | solution.py:267
  21.2 2.8 %collective-permute-start.2 = (bf16[16,64,256]{2,1,0:T(8,128)(2,1)S(1)}, bf16[16,64,256]{2,1,0:T(8,128)(2,1)S(1)}, u32[]{:S(2)}, u32[]{:S(2)}) collective-permute-start(bf16[16,64,256]{2,1,0:T(8,128)(2,1)S(1)} %get-tuple-element.50), channel_id=1, source_target_pairs={{0,1},{1,2},{2,3},{3,4},{4,5},{5,6},{6,7},{7,8},{8,9},{9,10},{10,1... | collective-permute-start | bytes 1572872 | tf_op jit(solution)/shard_map/ppermute | solution.py:266
  24.0 0.0 collective-permute-done.before
  24.0 0.0 collective-permute-done.1.after
  24.0 0.0 copy-done.1
  24.0 0.0 copy-done.2
  24.0 11.2 %forward.1 = (bf16[1024,256]{1,0:T(8,128)(2,1)}, bf16[2304,256]{1,0:T(8,128)(2,1)S(1)}) custom-call(s32[16]{0:T(128)S(1)} %copy-done.4, s32[16,6]{1,0:T(8,128)S(1)} %copy.11.rows, s32[16,6]{1,0:T(8,128)S(1)} %copy.12.offs, bf16[16,64,256]{2,1,0:T(8,128)(2,1)S(1)} %collective-permute-done.before, bf16[16,64,256]{2,1,0:T(8,128)(2,1)S(1)} %copy-done.2, ...), custom_call_target="tpu_custom_call" | custom-call | flops 8000000000 | bytes 8000000 | tf_op jit(solution)/shard_map/forward/pallas_call | solution.py:212
  35.2 29.3 %weight_sum.1 = bf16[2,2,4,144,256]{4,3,2,1,0:T(8,128)(2,1)S(1)} custom-call(bf16[2,2,4,144,256]{4,3,2,1,0:T(8,128)(2,1)S(1)} %bitcast.9), custom_call_target="tpu_custom_call" | custom-call | flops 30000001024 | bytes 60000000 | tf_op jit(solution)/shard_map/weight_sum/pallas_call | solution.py:249
  64.5 1.6 %convert_multiply_fusion = f32[2,2,4,144,256]{4,3,2,1,0:T(8,128)} fusion(bf16[2,2,4,144,256]{4,3,2,1,0:T(8,128)(2,1)S(1)} %weight_sum.1), kind=kLoop, calls=%fused_computation | loop fusion | flops 1179648 | bytes 3538944 | tf_op jit(solution)/shard_map/mul | solution.py:265
  66.1 0.0 collective-permute-done.3
  66.1 0.0 collective-permute-done.2
  66.1 1.2 %convert_add_fusion = f32[16,64,256]{2,1,0:T(8,128)} fusion(bf16[16,64,256]{2,1,0:T(8,128)(2,1)S(1)} %collective-permute-done.3, f32[16,64,256]{2,1,0:T(8,128)S(1)} %get-tuple-element.49, bf16[16,64,256]{2,1,0:T(8,128)(2,1)S(1)} %collective-permute-done.2), kind=kLoop, calls=%fused_computation.1 | loop fusion | flops 1048576 | bytes 3145728 | tf_op jit(solution)/shard_map/add | solution.py:269
  (3 shorter events, 0.0 us)
Async XLA Ops:
  0.6 23.3 %collective-permute-start = (bf16[16,64,256]{2,1,0:T(8,128)(2,1)}, bf16[16,64,256]{2,1,0:T(8,128)(2,1)S(1)}, u32[]{:S(2)}, u32[]{:S(2)}) collective-permute-start(bf16[16,64,256]{2,1,0:T(8,128)(2,1)} %source.1), channel_id=1, source_target_pairs={{0,1},{1,2},{2,3},{3,4},{4,5},{5,6},{6,7},{7,8},{8,9},{9,10},{10,1... | collective-permute-start | bytes 1572872 | tf_op jit(solution)/shard_map/ppermute | solution.py:204
  0.7 23.3 %collective-permute-start.1 = (bf16[16,64,256]{2,1,0:T(8,128)(2,1)}, bf16[16,64,256]{2,1,0:T(8,128)(2,1)S(1)}, u32[]{:S(2)}, u32[]{:S(2)}) collective-permute-start(bf16[16,64,256]{2,1,0:T(8,128)(2,1)} %source.1), channel_id=1, source_target_pairs={{1,0},{2,1},{3,2},{4,3},{5,4},{6,5},{7,6},{8,7},{9,8},{10,9},{11,1... | collective-permute-start | bytes 1572872 | tf_op jit(solution)/shard_map/ppermute | solution.py:205
  4.0 1.3 %copy-start = (bf16[9,256,256]{2,1,0:T(8,128)(2,1)S(1)}, bf16[9,256,256]{2,1,0:T(8,128)(2,1)}, u32[]{:S(2)}) copy-start(bf16[9,256,256]{2,1,0:T(8,128)(2,1)} %param.20) | copy-start | bytes 3538948
  5.3 1.0 %copy-start.3 = (bf16[16,64,256]{2,1,0:T(8,128)(2,1)S(1)}, bf16[16,64,256]{2,1,0:T(8,128)(2,1)}, u32[]{:S(2)}) copy-start(bf16[16,64,256]{2,1,0:T(8,128)(2,1)} %param.21) | copy-start | bytes 1572868
  6.4 0.7 copy-start.4
  7.0 17.0 %copy-start.1 = (bf16[9,256,256]{2,1,0:T(8,128)(2,1)S(1)}, bf16[9,256,256]{2,1,0:T(8,128)(2,1)}, u32[]{:S(2)}) copy-start(bf16[9,256,256]{2,1,0:T(8,128)(2,1)} %param.20) | copy-start | bytes 3538948
  7.0 17.0 %copy-start.2 = (bf16[16,64,256]{2,1,0:T(8,128)(2,1)S(1)}, bf16[16,64,256]{2,1,0:T(8,128)(2,1)}, u32[]{:S(2)}) copy-start(bf16[16,64,256]{2,1,0:T(8,128)(2,1)} %source.1) | copy-start | bytes 1572868
  19.5 46.7 %collective-permute-start.3 = (bf16[16,64,256]{2,1,0:T(8,128)(2,1)S(1)}, bf16[16,64,256]{2,1,0:T(8,128)(2,1)S(1)}, u32[]{:S(2)}, u32[]{:S(2)}) collective-permute-start(bf16[16,64,256]{2,1,0:T(8,128)(2,1)S(1)} %get-tuple-element.51), channel_id=1, source_target_pairs={{1,0},{2,1},{3,2},{4,3},{5,4},{6,5},{7,6},{8,7},{9,8},{10,9},{11,1... | collective-permute-start | bytes 1572872 | tf_op jit(solution)/shard_map/ppermute | solution.py:267
  21.2 44.9 %collective-permute-start.2 = (bf16[16,64,256]{2,1,0:T(8,128)(2,1)S(1)}, bf16[16,64,256]{2,1,0:T(8,128)(2,1)S(1)}, u32[]{:S(2)}, u32[]{:S(2)}) collective-permute-start(bf16[16,64,256]{2,1,0:T(8,128)(2,1)S(1)} %get-tuple-element.50), channel_id=1, source_target_pairs={{0,1},{1,2},{2,3},{3,4},{4,5},{5,6},{6,7},{7,8},{8,9},{9,10},{10,1... | collective-permute-start | bytes 1572872 | tf_op jit(solution)/shard_map/ppermute | solution.py:266

commit v4 on v3

--- a/solution.py
+++ b/solution.py
@@ -27,7 +27,7 @@
             band[k * cols : (k + 1) * cols, b * 128 : (b + 1) * 128] = wide.astype(jnp.bfloat16)
 
 
-def forward_kernel(counts, rows, offs, before, source, after, quad, weight, cot, mixed, grad, ext, band, picked, basis):
+def forward_kernel(counts, rows, offs, before, source, after, quad, basis, ext, band, picked):
     lat, cols, ch = source.shape
     filters = quad.shape[0]
     blocks = rows.shape[1]
@@ -57,22 +57,9 @@
         return 0
 
     lax.fori_loop(0, lat, step, 0)
-    total = lat * cols
-    tile = 256
-
-    def mix(m, _):
-        here = pl.ds(pl.multiple_of(m * tile, tile), tile)
-        mixed[here, :] = jnp.dot(basis[here, :], weight[...], preferred_element_type=jnp.float32).astype(jnp.bfloat16)
-        return 0
-
-    lax.fori_loop(0, total // tile, mix, 0)
-    for k in range(filters):
-        here = slice(k * ch, (k + 1) * ch)
-        grad[here, :] = lax.dot_general(
-            basis[:, here], cot[...], (((0,), (0,)), ((), ())), preferred_element_type=jnp.float32
-        ).astype(jnp.bfloat16)
-    if grad.shape[0] > filters * ch:
-        grad[filters * ch :, :] = jnp.zeros((grad.shape[0] - filters * ch, ch), jnp.bfloat16)
+    spare = basis.shape[1] - filters * ch
+    if spare > 0:
+        basis[:, filters * ch :] = jnp.zeros((lat * cols, spare), jnp.bfloat16)
 
 
 def backward_kernel(counts, rows, offs, quad, weight, cot, inner, west, east, total, band, grads):
@@ -117,7 +104,7 @@
     east[...] = total[:, reach + cols : 2 * reach + cols, :].astype(jnp.bfloat16)
 
 
-def sum_kernel(mine, out, paired, half, level, partial, others, sems):
+def sum_kernel(basis, weight, cot, mixed, out, mine, paired, half, level, partial, others, sems):
     groups, rows, ch = partial.shape
     me = lax.axis_index("lon")
     core = lax.rem(me, 2)
@@ -144,12 +131,23 @@
         copy.start()
         return copy
 
+    def term(half):
+        width = 2 * groups * rows
+        here = pl.ds(pl.multiple_of(half * width, 128), width)
+        part = lax.dot_general(
+            basis[:, here], cot[...], (((0,), (0,)), ((), ())), preferred_element_type=jnp.float32
+        )
+        mine[half] = part.astype(jnp.bfloat16).reshape(2, groups, rows, ch)
+
+    term(1 - core)
     order = list(range(1, groups)) + [0]
     line = [side, 1 - side]
     pairs = {}
     for t in (1, 0):
         for d in order:
             pairs[t, d] = send(mine.at[1 - core, line[t], spot[d]], paired.at[t, d], 0, t * groups + d, sibling)
+
+    term(core)
 
     def both(t, d):
         pairs[t, d].wait()
@@ -167,6 +165,15 @@
         if d > 0:
             partial[d] = own.astype(jnp.bfloat16)
             crossing[d] = send(partial.at[d], others.at[d], 2, d, peer[d])
+    tile = 256
+
+    def mix(m, _):
+        here = pl.ds(pl.multiple_of(m * tile, tile), tile)
+        known = basis[here, : weight.shape[0]]
+        mixed[here, :] = jnp.dot(known, weight[...], preferred_element_type=jnp.float32).astype(jnp.bfloat16)
+        return 0
+
+    lax.fori_loop(0, mixed.shape[0] // tile, mix, 0)
     for d in range(1, groups):
         crossing[d].wait()
         own = own + others[d].astype(jnp.float32)
@@ -209,24 +216,20 @@
     params = pltpu.CompilerParams(vmem_limit_bytes=48 * 2**20)
     chunk = -(-filters * ch // (16 * peers)) * 16
     wide = cols + 2 * reach + 8
-    mixed, local = pl.pallas_call(
+    basis = pl.pallas_call(
         forward_kernel,
-        out_shape=[
-            jax.ShapeDtypeStruct((lat * cols, ch), jnp.bfloat16),
-            jax.ShapeDtypeStruct((peers * chunk, ch), jnp.bfloat16),
-        ],
-        in_specs=[SM] * 3 + [VM] * 6,
-        out_specs=[VM] * 2,
+        out_shape=jax.ShapeDtypeStruct((lat * cols, peers * chunk), jnp.bfloat16),
+        in_specs=[SM] * 3 + [VM] * 4,
+        out_specs=VM,
         scratch_shapes=[
             pltpu.VMEM((lat, wide, ch), jnp.float32),
             pltpu.VMEM((filters * cols, blocks * 128), jnp.bfloat16),
             pltpu.VMEM((blocks * 128, ch), jnp.bfloat16),
-            pltpu.VMEM((lat * cols, filters * ch), jnp.bfloat16),
-        ],
-        compiler_params=params,
+        ],
+        compiler_params=pltpu.CompilerParams(vmem_limit_bytes=32 * 2**20),
         cost_estimate=pl.CostEstimate(flops=8_000_000_000, bytes_accessed=8_000_000, transcendentals=0),
         name="forward",
-    )(counts, block_rows, offsets, before, source, after, quad, flat_weight, flat_cot)
+    )(counts, block_rows, offsets, before, source, after, quad)
     inner, west, east = pl.pallas_call(
         backward_kernel,
         out_shape=[
@@ -246,12 +249,16 @@
         name="backward",
     )(counts, block_rows, offsets, quad, flat_weight, flat_cot)
     groups = peers // 4
-    summed = pl.pallas_call(
+    mixed, summed = pl.pallas_call(
         sum_kernel,
-        out_shape=jax.ShapeDtypeStruct((2, 2, groups, chunk, ch), jnp.bfloat16),
-        in_specs=[VM],
-        out_specs=VM,
-        scratch_shapes=[pltpu.VMEM((2, groups, chunk, ch), jnp.bfloat16)]
+        out_shape=[
+            jax.ShapeDtypeStruct((lat * cols, ch), jnp.bfloat16),
+            jax.ShapeDtypeStruct((2, 2, groups, chunk, ch), jnp.bfloat16),
+        ],
+        in_specs=[VM] * 3,
+        out_specs=[VM] * 2,
+        scratch_shapes=[pltpu.VMEM((2, 2, groups, chunk, ch), jnp.bfloat16)]
+        + [pltpu.VMEM((2, groups, chunk, ch), jnp.bfloat16)]
         + [pltpu.VMEM((groups, chunk, ch), jnp.bfloat16)] * 4
         + [pltpu.SemaphoreType.DMA((6, 2, 2 * groups))],
         compiler_params=pltpu.CompilerParams(
@@ -259,7 +266,7 @@
         ),
         cost_estimate=pl.CostEstimate(flops=30_000_000_000, bytes_accessed=60_000_000, transcendentals=0),
         name="weight_sum",
-    )(local.reshape(2, 2, groups, chunk, ch))
+    )(basis, flat_weight, flat_cot)
     summed = summed.reshape(peers * chunk, ch)[: filters * ch].astype(jnp.float32)
     factor = 1.0 / math.sqrt(lat * cols * peers)
     grad_weight = (summed * factor).reshape(filters, ch, ch)

time: 68.4 us -> 69.1 us (1.010)
  local copies, waits for them, and re-layouts: 5.51 us -> 6.3 us
    pallas_call x2, Pallas kernels: 40.5 us -> 38.8 us  [the longest x1 30.7 us: shards(): pl.pallas_call(sum_kernel, out_shape=[jax.ShapeDtypeStruct((lat * cols, c...]
    pallas_call x1, Pallas kernels: 12.4 us -> 14.1 us  [shards(): pl.pallas_call(backward_kernel, out_shape=[jax.ShapeDtypeStruct((lat, col...]
    unnamed x13 -> x12, local copies, waits for them, and re-layouts: 5.51 us -> 6.3 us
  transfers between devices with their start and end apart: 4 -> 4, of which waited for: 0 -> 0; matrix products, arithmetic and copies ran while one was open for 6% -> 6% of each run, Pallas kernels for 79% -> 78%
where the time goes in v4:
time: 69.1 us; the launch traced here: 68 us
  Pallas kernels  52.8 us (76%)
  local copies, waits for them, and re-layouts  6.3 us (9%)
  starting transfers between devices  5.28 us (8%)
  other arithmetic  2.9 us (4%)
    pallas_call x1, Pallas kernels, shards(): pl.pallas_call(sum_kernel, out_shape=[jax.ShapeDtypeStruct((lat * cols, c...  30.7 us
    pallas_call x1, Pallas kernels, shards(): pl.pallas_call(backward_kernel, out_shape=[jax.ShapeDtypeStruct((lat, col...  14.1 us
    pallas_call x1, Pallas kernels, shards(): pl.pallas_call(forward_kernel, out_shape=jax.ShapeDtypeStruct((lat * cols...  8.05 us
    unnamed x12, local copies, waits for them, and re-layouts  6.3 us
    ppermute x1, starting transfers between devices, shards(): west_in = lax.ppermute(east, 'lon', up).astype(jnp.float32)  2.77 us
    ppermute x1, starting transfers between devices, shards(): east_in = lax.ppermute(west, 'lon', down).astype(jnp.float32)  1.73 us
    mul x1, other arithmetic, shards(): grad_weight = (summed * factor).reshape(filters, ch, ch)  1.65 us
  transfers between devices with their start and end apart: 4, of which 0 were waited for; matrix products, arithmetic and copies ran while one was open for 6% of the time, Pallas kernels for 78%

profile of v4, /device:TPU:29, one launch (start us, length us, event | category | flops | bytes accessed | tf_op | source)
XLA Modules:
  0.0 68.0 jit_solution(9293337758825149985)
XLA Ops:
  0.6 0.1 collective-permute-start
  0.7 0.7 %collective-permute-start.1 = (bf16[16,64,256]{2,1,0:T(8,128)(2,1)}, bf16[16,64,256]{2,1,0:T(8,128)(2,1)S(1)}, u32[]{:S(2)}, u32[]{:S(2)}) collective-permute-start(bf16[16,64,256]{2,1,0:T(8,128)(2,1)} %source.1), channel_id=1, source_target_pairs={{1,0},{2,1},{3,2},{4,3},{5,4},{6,5},{7,6},{8,7},{9,8},{10,9},{11,1... | collective-permute-start | bytes 1572872 | tf_op jit(solution)/shard_map/ppermute | solution.py:212
  1.4 0.8 %copy.11.rows = s32[16,6]{1,0:T(8,128)S(1)} copy(s32[16,6]{0,1:T(8,128)} %param.17) | data formatting | bytes 768 | tf_op args[2]
  2.2 0.8 %copy.12.offs = s32[16,6]{1,0:T(8,128)S(1)} copy(s32[16,6]{0,1:T(8,128)} %param.18) | data formatting | bytes 768 | tf_op args[3]
  3.0 1.0 %copy.10 = bf16[9,16,6,64]{3,2,1,0:T(8,128)(2,1)S(1)} copy(bf16[9,16,6,64]{3,1,2,0:T(8,128)(2,1)} %param.16) | data formatting | bytes 221184 | tf_op args[1]
  4.0 0.1 pad_convert_fusion.quad
  4.0 0.0 copy-start
  4.0 1.3 %copy-done = bf16[9,256,256]{2,1,0:T(8,128)(2,1)S(1)} copy-done((bf16[9,256,256]{2,1,0:T(8,128)(2,1)S(1)}, bf16[9,256,256]{2,1,0:T(8,128)(2,1)}, u32[]{:S(2)}) %copy-start) | copy-done | bytes 1179672
  5.3 0.0 copy-start.2
  5.3 1.0 %copy-done.2 = bf16[16,64,256]{2,1,0:T(8,128)(2,1)S(1)} copy-done((bf16[16,64,256]{2,1,0:T(8,128)(2,1)S(1)}, bf16[16,64,256]{2,1,0:T(8,128)(2,1)}, u32[]{:S(2)}) %copy-start.2) | copy-done | bytes 524312
  6.4 0.7 copy-done.3
  7.0 14.1 %backward.1 = (f32[16,64,256]{2,1,0:T(8,128)S(1)}, bf16[16,64,256]{2,1,0:T(8,128)(2,1)S(1)}, bf16[16,64,256]{2,1,0:T(8,128)(2,1)S(1)}) custom-call(s32[16]{0:T(128)S(1)} %copy-done.3, s32[16,6]{1,0:T(8,128)S(1)} %copy.11.rows, s32[16,6]{1,0:T(8,128)S(1)} %copy.12.offs, f32[9,16,6,128]{3,2,1,0:T(8,128)S(1)} %pad_convert_fusion.quad, ...), custom_call_target="tpu_custom_call" | custom-call | flops 8000000000 | bytes 8000000 | tf_op jit(solution)/shard_map/backward/pallas_call | solution.py:233
  21.1 1.7 %collective-permute-start.3 = (bf16[16,64,256]{2,1,0:T(8,128)(2,1)S(1)}, bf16[16,64,256]{2,1,0:T(8,128)(2,1)S(1)}, u32[]{:S(2)}, u32[]{:S(2)}) collective-permute-start(bf16[16,64,256]{2,1,0:T(8,128)(2,1)S(1)} %get-tuple-element.51), channel_id=1, source_target_pairs={{1,0},{2,1},{3,2},{4,3},{5,4},{6,5},{7,6},{8,7},{9,8},{10,9},{11,1... | collective-permute-start | bytes 1572872 | tf_op jit(solution)/shard_map/ppermute | solution.py:274
  22.8 2.8 %collective-permute-start.2 = (bf16[16,64,256]{2,1,0:T(8,128)(2,1)S(1)}, bf16[16,64,256]{2,1,0:T(8,128)(2,1)S(1)}, u32[]{:S(2)}, u32[]{:S(2)}) collective-permute-start(bf16[16,64,256]{2,1,0:T(8,128)(2,1)S(1)} %get-tuple-element.50), channel_id=1, source_target_pairs={{0,1},{1,2},{2,3},{3,4},{4,5},{5,6},{6,7},{7,8},{8,9},{9,10},{10,1... | collective-permute-start | bytes 1572872 | tf_op jit(solution)/shard_map/ppermute | solution.py:273
  25.6 0.0 collective-permute-done.before
  25.6 0.0 collective-permute-done.1.after
  25.6 0.0 copy-done.1
  25.6 8.1 %forward.1.basis = bf16[1024,2304]{1,0:T(8,128)(2,1)S(1)} custom-call(s32[16]{0:T(128)S(1)} %copy-done.3, s32[16,6]{1,0:T(8,128)S(1)} %copy.11.rows, s32[16,6]{1,0:T(8,128)S(1)} %copy.12.offs, bf16[16,64,256]{2,1,0:T(8,128)(2,1)S(1)} %collective-permute-done.before, bf16[16,64,256]{2,1,0:T(8,128)(2,1)S(1)} %copy-done.1, ...), custom_call_target="tpu_custom_call" | custom-call | flops 8000000000 | bytes 8000000 | tf_op jit(solution)/shard_map/forward/pallas_call | solution.py:219
  33.6 30.7 %weight_sum.1 = (bf16[1024,256]{1,0:T(8,128)(2,1)S(1)}, bf16[2,2,4,144,256]{4,3,2,1,0:T(8,128)(2,1)S(1)}) custom-call(bf16[1024,2304]{1,0:T(8,128)(2,1)S(1)} %forward.1.basis, bf16[2304,256]{1,0:T(8,128)(2,1)S(1)} %bitcast.6, bf16[1024,256]{1,0:T(8,128)(2,1)S(1)} %bitcast.8), custom_call_target="tpu_custom_call" | custom-call | flops 30000001024 | bytes 60000000 | tf_op jit(solution)/shard_map/weight_sum/pallas_call | solution.py:252
  64.4 1.6 %convert_multiply_fusion = f32[2,2,4,144,256]{4,3,2,1,0:T(8,128)} fusion(bf16[2,2,4,144,256]{4,3,2,1,0:T(8,128)(2,1)S(1)} %get-tuple-element.52), kind=kLoop, calls=%fused_computation | loop fusion | flops 1179648 | bytes 3538944 | tf_op jit(solution)/shard_map/mul | solution.py:272
  66.0 0.0 collective-permute-done.3
  66.0 0.0 collective-permute-done.2
  66.0 1.2 %convert_add_fusion = f32[16,64,256]{2,1,0:T(8,128)} fusion(bf16[16,64,256]{2,1,0:T(8,128)(2,1)S(1)} %collective-permute-done.3, f32[16,64,256]{2,1,0:T(8,128)S(1)} %get-tuple-element.49, bf16[16,64,256]{2,1,0:T(8,128)(2,1)S(1)} %collective-permute-done.2), kind=kLoop, calls=%fused_computation.1 | loop fusion | flops 1048576 | bytes 3145728 | tf_op jit(solution)/shard_map/add | solution.py:276
  67.2 0.8 %copy.16 = bf16[16,64,256]{2,1,0:T(8,128)(2,1)} copy(bf16[16,64,256]{2,1,0:T(8,128)(2,1)S(1)} %bitcast.4) | data formatting | bytes 1048576
  (2 shorter events, 0.0 us)
Async XLA Ops:
  0.6 25.0 %collective-permute-start = (bf16[16,64,256]{2,1,0:T(8,128)(2,1)}, bf16[16,64,256]{2,1,0:T(8,128)(2,1)S(1)}, u32[]{:S(2)}, u32[]{:S(2)}) collective-permute-start(bf16[16,64,256]{2,1,0:T(8,128)(2,1)} %source.1), channel_id=1, source_target_pairs={{0,1},{1,2},{2,3},{3,4},{4,5},{5,6},{6,7},{7,8},{8,9},{9,10},{10,1... | collective-permute-start | bytes 1572872 | tf_op jit(solution)/shard_map/ppermute | solution.py:211
  0.7 24.9 %collective-permute-start.1 = (bf16[16,64,256]{2,1,0:T(8,128)(2,1)}, bf16[16,64,256]{2,1,0:T(8,128)(2,1)S(1)}, u32[]{:S(2)}, u32[]{:S(2)}) collective-permute-start(bf16[16,64,256]{2,1,0:T(8,128)(2,1)} %source.1), channel_id=1, source_target_pairs={{1,0},{2,1},{3,2},{4,3},{5,4},{6,5},{7,6},{8,7},{9,8},{10,9},{11,1... | collective-permute-start | bytes 1572872 | tf_op jit(solution)/shard_map/ppermute | solution.py:212
  4.0 1.3 %copy-start = (bf16[9,256,256]{2,1,0:T(8,128)(2,1)S(1)}, bf16[9,256,256]{2,1,0:T(8,128)(2,1)}, u32[]{:S(2)}) copy-start(bf16[9,256,256]{2,1,0:T(8,128)(2,1)} %param.20) | copy-start | bytes 3538948
  5.3 1.0 %copy-start.2 = (bf16[16,64,256]{2,1,0:T(8,128)(2,1)S(1)}, bf16[16,64,256]{2,1,0:T(8,128)(2,1)}, u32[]{:S(2)}) copy-start(bf16[16,64,256]{2,1,0:T(8,128)(2,1)} %param.21) | copy-start | bytes 1572868
  6.4 0.7 copy-start.3
  7.0 18.6 %copy-start.1 = (bf16[16,64,256]{2,1,0:T(8,128)(2,1)S(1)}, bf16[16,64,256]{2,1,0:T(8,128)(2,1)}, u32[]{:S(2)}) copy-start(bf16[16,64,256]{2,1,0:T(8,128)(2,1)} %source.1) | copy-start | bytes 1572868
  21.1 44.9 %collective-permute-start.3 = (bf16[16,64,256]{2,1,0:T(8,128)(2,1)S(1)}, bf16[16,64,256]{2,1,0:T(8,128)(2,1)S(1)}, u32[]{:S(2)}, u32[]{:S(2)}) collective-permute-start(bf16[16,64,256]{2,1,0:T(8,128)(2,1)S(1)} %get-tuple-element.51), channel_id=1, source_target_pairs={{1,0},{2,1},{3,2},{4,3},{5,4},{6,5},{7,6},{8,7},{9,8},{10,9},{11,1... | collective-permute-start | bytes 1572872 | tf_op jit(solution)/shard_map/ppermute | solution.py:274
  22.8 43.2 %collective-permute-start.2 = (bf16[16,64,256]{2,1,0:T(8,128)(2,1)S(1)}, bf16[16,64,256]{2,1,0:T(8,128)(2,1)S(1)}, u32[]{:S(2)}, u32[]{:S(2)}) collective-permute-start(bf16[16,64,256]{2,1,0:T(8,128)(2,1)S(1)} %get-tuple-element.50), channel_id=1, source_target_pairs={{0,1},{1,2},{2,3},{3,4},{4,5},{5,6},{6,7},{7,8},{8,9},{9,10},{10,1... | collective-permute-start | bytes 1572872 | tf_op jit(solution)/shard_map/ppermute | solution.py:273

commit v5 on v4

--- a/solution.py
+++ b/solution.py
@@ -21,7 +21,7 @@
     for b in range(blocks):
         live = (b < counts[i]).astype(jnp.float32)
         for k in range(filters):
-            row = quad[k, i, pl.ds(b, 1), :] * live
+            row = quad[k, b, pl.ds(i, 1), :] * live
             wide = jnp.broadcast_to(row, (cols, row.shape[1]))
             wide = pltpu.roll(wide, 0, 1, stride=1, stride_axis=0)
             band[k * cols : (k + 1) * cols, b * 128 : (b + 1) * 128] = wide.astype(jnp.bfloat16)
@@ -30,7 +30,7 @@
 def forward_kernel(counts, rows, offs, before, source, after, quad, basis, ext, band, picked):
     lat, cols, ch = source.shape
     filters = quad.shape[0]
-    blocks = rows.shape[1]
+    blocks = rows.shape[0]
     reach = before.shape[1]
     ext[:, :reach, :] = before[...].astype(jnp.float32)
     ext[:, reach : reach + cols, :] = source[...].astype(jnp.float32)
@@ -39,9 +39,9 @@
     def live_step(i, blocks):
         build_band(i, counts, quad, band, filters, blocks, cols)
         for b in range(blocks):
-            start = offs[i, b] + reach
+            start = offs[b, i] + reach
             shift = start % 8
-            near = ext[rows[i, b], pl.ds(pl.multiple_of(start - shift, 8), 136), :].reshape(17, 8, ch)
+            near = ext[rows[b, i], pl.ds(pl.multiple_of(start - shift, 8), 136), :].reshape(17, 8, ch)
             near = pltpu.roll(near, (8 - shift) % 8, 1)
             place = lax.broadcasted_iota(jnp.int32, (16, 8, ch), 1)
             near = jnp.where(place < 8 - shift, near[:16], near[1:]).reshape(128, ch)
@@ -65,7 +65,7 @@
 def backward_kernel(counts, rows, offs, quad, weight, cot, inner, west, east, total, band, grads):
     lat, cols, ch = inner.shape
     filters = quad.shape[0]
-    blocks = rows.shape[1]
+    blocks = rows.shape[0]
     reach = west.shape[1]
     total[...] = jnp.zeros_like(total)
     for k in range(filters):
@@ -83,7 +83,7 @@
             band[:, : blocks * 128], grads[i], (((0,), (0,)), ((), ())), preferred_element_type=jnp.float32
         )
         for b in range(blocks):
-            start = offs[i, b] + reach
+            start = offs[b, i] + reach
             shift = start % 8
             far = pltpu.roll(parts[b * 128 : (b + 1) * 128].reshape(16, 8, ch), shift, 1)
             zero = jnp.zeros((1, 8, ch), jnp.float32)
@@ -92,7 +92,7 @@
                 place >= shift, jnp.concatenate([far, zero], axis=0), jnp.concatenate([zero, far], axis=0)
             )
             here = pl.ds(pl.multiple_of(start - shift, 8), 136)
-            total[rows[i, b], here, :] += far.reshape(136, ch)
+            total[rows[b, i], here, :] += far.reshape(136, ch)
 
     def step(i, _):
         by_count(counts[i], blocks, lambda n: live_step(i, n))
@@ -210,7 +210,7 @@
     down = [(j, i) for i, j in up]
     before = lax.ppermute(source[:, cols - reach :], "lon", up)
     after = lax.ppermute(source[:, :reach], "lon", down)
-    quad = jnp.pad(quadrature.astype(jnp.float32), ((0, 0), (0, 0), (0, 0), (0, 128 - reach)))
+    quad = jnp.pad(quadrature.transpose(0, 2, 1, 3).astype(jnp.float32), ((0, 0), (0, 0), (0, 0), (0, 128 - reach)))
     flat_weight = weight.reshape(filters * ch, ch)
     flat_cot = cotangent.reshape(lat * cols, ch)
     params = pltpu.CompilerParams(vmem_limit_bytes=48 * 2**20)
@@ -229,7 +229,7 @@
         compiler_params=pltpu.CompilerParams(vmem_limit_bytes=32 * 2**20),
         cost_estimate=pl.CostEstimate(flops=8_000_000_000, bytes_accessed=8_000_000, transcendentals=0),
         name="forward",
-    )(counts, block_rows, offsets, before, source, after, quad)
+    )(counts, block_rows.T, offsets.T, before, source, after, quad)
     inner, west, east = pl.pallas_call(
         backward_kernel,
         out_shape=[
@@ -247,7 +247,7 @@
         compiler_params=params,
         cost_estimate=pl.CostEstimate(flops=8_000_000_000, bytes_accessed=8_000_000, transcendentals=0),
         name="backward",
-    )(counts, block_rows, offsets, quad, flat_weight, flat_cot)
+    )(counts, block_rows.T, offsets.T, quad, flat_weight, flat_cot)
     groups = peers // 4
     mixed, summed = pl.pallas_call(
         sum_kernel,

time: 69.1 us -> 67.1 us (0.971)
  Pallas kernels: 52.8 us -> 51.5 us
  local copies, waits for them, and re-layouts: 6.3 us -> 5.13 us
  other arithmetic: 2.9 us -> 3.81 us
    unnamed x12 -> x13, local copies, waits for them, and re-layouts: 6.3 us -> 5.13 us
    pad x1, other arithmetic: 0.06 us -> 0.97 us  [shards(): jnp.pad(quadrature.transpose(0, 2, 1, 3).astype(jnp.float32), ((0, 0), (0...]
    pallas_call x1, Pallas kernels: 14.1 us -> 13.2 us  [shards(): pl.pallas_call(backward_kernel, out_shape=[jax.ShapeDtypeStruct((lat, col...]
  transfers between devices with their start and end apart: 4 -> 4, of which waited for: 0 -> 0; matrix products, arithmetic and copies ran while one was open for 6% -> 4% of each run, Pallas kernels for 78% -> 77%
where the time goes in v5:
time: 67.1 us; the launch traced here: 66.4 us
  Pallas kernels  51.5 us (77%)
  starting transfers between devices  5.28 us (8%)
  local copies, waits for them, and re-layouts  5.13 us (8%)
  other arithmetic  3.81 us (6%)
  between operations  0.69 us (1%)
    pallas_call x1, Pallas kernels, shards(): pl.pallas_call(sum_kernel, out_shape=[jax.ShapeDtypeStruct((lat * cols, c...  30.7 us
    pallas_call x1, Pallas kernels, shards(): pl.pallas_call(backward_kernel, out_shape=[jax.ShapeDtypeStruct((lat, col...  13.2 us
    pallas_call x1, Pallas kernels, shards(): pl.pallas_call(forward_kernel, out_shape=jax.ShapeDtypeStruct((lat * cols...  7.53 us
    unnamed x13, local copies, waits for them, and re-layouts  5.13 us
    ppermute x1, starting transfers between devices, shards(): west_in = lax.ppermute(east, 'lon', up).astype(jnp.float32)  2.78 us
    ppermute x1, starting transfers between devices, shards(): east_in = lax.ppermute(west, 'lon', down).astype(jnp.float32)  1.72 us
    mul x1, other arithmetic, shards(): grad_weight = (summed * factor).reshape(filters, ch, ch)  1.65 us
  transfers between devices with their start and end apart: 4, of which 0 were waited for; matrix products, arithmetic and copies ran while one was open for 4% of the time, Pallas kernels for 77%

profile of v5, /device:TPU:29, one launch (start us, length us, event | category | flops | bytes accessed | tf_op | source)
XLA Modules:
  0.0 66.4 jit_solution(8653010240717564482)
XLA Ops:
  0.6 0.1 collective-permute-start
  0.7 0.7 %collective-permute-start.1 = (bf16[16,64,256]{2,1,0:T(8,128)(2,1)}, bf16[16,64,256]{2,1,0:T(8,128)(2,1)S(1)}, u32[]{:S(2)}, u32[]{:S(2)}) collective-permute-start(bf16[16,64,256]{2,1,0:T(8,128)(2,1)} %source.1), channel_id=1, source_target_pairs={{1,0},{2,1},{3,2},{4,3},{5,4},{6,5},{7,6},{8,7},{9,8},{10,9},{11,1... | collective-permute-start | bytes 1572872 | tf_op jit(solution)/shard_map/ppermute | solution.py:212
  1.4 1.0 %pad_convert_fusion.quad = f32[9,6,16,128]{3,2,1,0:T(8,128)S(1)} fusion(bf16[9,6,16,64]{3,2,1,0:T(8,128)(2,1)} %bitcast.17), kind=kLoop, calls=%fused_computation.2 | loop fusion | flops 110592 | bytes 552960 | tf_op jit(solution)/shard_map/jit(_pad)/pad | solution.py:213
  2.4 0.0 copy-start
  2.4 1.3 %copy-done = bf16[9,256,256]{2,1,0:T(8,128)(2,1)S(1)} copy-done((bf16[9,256,256]{2,1,0:T(8,128)(2,1)S(1)}, bf16[9,256,256]{2,1,0:T(8,128)(2,1)}, u32[]{:S(2)}) %copy-start) | copy-done | bytes 1179672
  3.7 1.0 %copy-done.2 = bf16[16,64,256]{2,1,0:T(8,128)(2,1)S(1)} copy-done((bf16[16,64,256]{2,1,0:T(8,128)(2,1)S(1)}, bf16[16,64,256]{2,1,0:T(8,128)(2,1)}, u32[]{:S(2)}) %copy-start.2) | copy-done | bytes 524312
  4.7 0.0 copy-start.3
  4.7 0.7 %copy-done.3 = s32[16,6]{0,1:T(8,128)S(1)} copy-done((s32[16,6]{0,1:T(8,128)S(1)}, s32[16,6]{0,1:T(8,128)}, u32[]{:S(2)}) %copy-start.3) | copy-done | bytes 408
  5.4 0.0 copy-start.4
  5.4 0.7 %copy-done.4 = s32[16,6]{0,1:T(8,128)S(1)} copy-done((s32[16,6]{0,1:T(8,128)S(1)}, s32[16,6]{0,1:T(8,128)}, u32[]{:S(2)}) %copy-start.4) | copy-done | bytes 408
  6.1 0.7 copy-done.5
  6.8 13.2 %backward.1 = (f32[16,64,256]{2,1,0:T(8,128)S(1)}, bf16[16,64,256]{2,1,0:T(8,128)(2,1)S(1)}, bf16[16,64,256]{2,1,0:T(8,128)(2,1)S(1)}) custom-call(s32[16]{0:T(128)S(1)} %copy-done.5, s32[6,16]{1,0:T(8,128)S(1)} %bitcast.12, s32[6,16]{1,0:T(8,128)S(1)} %bitcast.14, f32[9,6,16,128]{3,2,1,0:T(8,128)S(1)} %pad_convert_fusion.quad, ...), custom_call_target="tpu_custom_call" | custom-call | flops 8000000000 | bytes 8000000 | tf_op jit(solution)/shard_map/backward/pallas_call | solution.py:233
  20.0 1.7 %collective-permute-start.3 = (bf16[16,64,256]{2,1,0:T(8,128)(2,1)S(1)}, bf16[16,64,256]{2,1,0:T(8,128)(2,1)S(1)}, u32[]{:S(2)}, u32[]{:S(2)}) collective-permute-start(bf16[16,64,256]{2,1,0:T(8,128)(2,1)S(1)} %get-tuple-element.51), channel_id=1, source_target_pairs={{1,0},{2,1},{3,2},{4,3},{5,4},{6,5},{7,6},{8,7},{9,8},{10,9},{11,1... | collective-permute-start | bytes 1572872 | tf_op jit(solution)/shard_map/ppermute | solution.py:274
  21.7 2.8 %collective-permute-start.2 = (bf16[16,64,256]{2,1,0:T(8,128)(2,1)S(1)}, bf16[16,64,256]{2,1,0:T(8,128)(2,1)S(1)}, u32[]{:S(2)}, u32[]{:S(2)}) collective-permute-start(bf16[16,64,256]{2,1,0:T(8,128)(2,1)S(1)} %get-tuple-element.50), channel_id=1, source_target_pairs={{0,1},{1,2},{2,3},{3,4},{4,5},{5,6},{6,7},{7,8},{8,9},{9,10},{10,1... | collective-permute-start | bytes 1572872 | tf_op jit(solution)/shard_map/ppermute | solution.py:273
  24.5 0.0 collective-permute-done.before
  24.5 0.0 collective-permute-done.1.after
  24.5 0.0 copy-done.1
  24.5 7.5 %forward.1.basis = bf16[1024,2304]{1,0:T(8,128)(2,1)S(1)} custom-call(s32[16]{0:T(128)S(1)} %copy-done.5, s32[6,16]{1,0:T(8,128)S(1)} %bitcast.13, s32[6,16]{1,0:T(8,128)S(1)} %bitcast.15, bf16[16,64,256]{2,1,0:T(8,128)(2,1)S(1)} %collective-permute-done.before, bf16[16,64,256]{2,1,0:T(8,128)(2,1)S(1)} %copy-done.1, ...), custom_call_target="tpu_custom_call" | custom-call | flops 8000000000 | bytes 8000000 | tf_op jit(solution)/shard_map/forward/pallas_call | solution.py:219
  32.0 30.7 %weight_sum.1 = (bf16[1024,256]{1,0:T(8,128)(2,1)S(1)}, bf16[2,2,4,144,256]{4,3,2,1,0:T(8,128)(2,1)S(1)}) custom-call(bf16[1024,2304]{1,0:T(8,128)(2,1)S(1)} %forward.1.basis, bf16[2304,256]{1,0:T(8,128)(2,1)S(1)} %bitcast.9, bf16[1024,256]{1,0:T(8,128)(2,1)S(1)} %bitcast.11), custom_call_target="tpu_custom_call" | custom-call | flops 30000001024 | bytes 60000000 | tf_op jit(solution)/shard_map/weight_sum/pallas_call | solution.py:252
  62.7 1.6 %convert_multiply_fusion = f32[2,2,4,144,256]{4,3,2,1,0:T(8,128)} fusion(bf16[2,2,4,144,256]{4,3,2,1,0:T(8,128)(2,1)S(1)} %get-tuple-element.52), kind=kLoop, calls=%fused_computation | loop fusion | flops 1179648 | bytes 3538944 | tf_op jit(solution)/shard_map/mul | solution.py:272
  64.4 0.0 collective-permute-done.3
  64.4 0.0 collective-permute-done.2
  64.4 1.2 %convert_add_fusion = f32[16,64,256]{2,1,0:T(8,128)} fusion(bf16[16,64,256]{2,1,0:T(8,128)(2,1)S(1)} %collective-permute-done.3, f32[16,64,256]{2,1,0:T(8,128)S(1)} %get-tuple-element.49, bf16[16,64,256]{2,1,0:T(8,128)(2,1)S(1)} %collective-permute-done.2), kind=kLoop, calls=%fused_computation.1 | loop fusion | flops 1048576 | bytes 3145728 | tf_op jit(solution)/shard_map/add | solution.py:276
  65.6 0.8 %copy.11 = bf16[16,64,256]{2,1,0:T(8,128)(2,1)} copy(bf16[16,64,256]{2,1,0:T(8,128)(2,1)S(1)} %bitcast.7) | data formatting | bytes 1048576
  (3 shorter events, 0.0 us)
Async XLA Ops:
  0.6 23.8 %collective-permute-start = (bf16[16,64,256]{2,1,0:T(8,128)(2,1)}, bf16[16,64,256]{2,1,0:T(8,128)(2,1)S(1)}, u32[]{:S(2)}, u32[]{:S(2)}) collective-permute-start(bf16[16,64,256]{2,1,0:T(8,128)(2,1)} %source.1), channel_id=1, source_target_pairs={{0,1},{1,2},{2,3},{3,4},{4,5},{5,6},{6,7},{7,8},{8,9},{9,10},{10,1... | collective-permute-start | bytes 1572872 | tf_op jit(solution)/shard_map/ppermute | solution.py:211
  0.7 23.8 %collective-permute-start.1 = (bf16[16,64,256]{2,1,0:T(8,128)(2,1)}, bf16[16,64,256]{2,1,0:T(8,128)(2,1)S(1)}, u32[]{:S(2)}, u32[]{:S(2)}) collective-permute-start(bf16[16,64,256]{2,1,0:T(8,128)(2,1)} %source.1), channel_id=1, source_target_pairs={{1,0},{2,1},{3,2},{4,3},{5,4},{6,5},{7,6},{8,7},{9,8},{10,9},{11,1... | collective-permute-start | bytes 1572872 | tf_op jit(solution)/shard_map/ppermute | solution.py:212
  2.4 1.3 %copy-start = (bf16[9,256,256]{2,1,0:T(8,128)(2,1)S(1)}, bf16[9,256,256]{2,1,0:T(8,128)(2,1)}, u32[]{:S(2)}) copy-start(bf16[9,256,256]{2,1,0:T(8,128)(2,1)} %param.20) | copy-start | bytes 3538948
  3.7 1.0 %copy-start.2 = (bf16[16,64,256]{2,1,0:T(8,128)(2,1)S(1)}, bf16[16,64,256]{2,1,0:T(8,128)(2,1)}, u32[]{:S(2)}) copy-start(bf16[16,64,256]{2,1,0:T(8,128)(2,1)} %param.21) | copy-start | bytes 1572868
  4.7 0.7 %copy-start.3 = (s32[16,6]{0,1:T(8,128)S(1)}, s32[16,6]{0,1:T(8,128)}, u32[]{:S(2)}) copy-start(s32[16,6]{0,1:T(8,128)} %param.17) | copy-start | bytes 1156
  5.4 0.7 %copy-start.4 = (s32[16,6]{0,1:T(8,128)S(1)}, s32[16,6]{0,1:T(8,128)}, u32[]{:S(2)}) copy-start(s32[16,6]{0,1:T(8,128)} %param.18) | copy-start | bytes 1156
  6.1 0.7 copy-start.5
  6.8 17.7 %copy-start.1 = (bf16[16,64,256]{2,1,0:T(8,128)(2,1)S(1)}, bf16[16,64,256]{2,1,0:T(8,128)(2,1)}, u32[]{:S(2)}) copy-start(bf16[16,64,256]{2,1,0:T(8,128)(2,1)} %source.1) | copy-start | bytes 1572868
  20.0 44.4 %collective-permute-start.3 = (bf16[16,64,256]{2,1,0:T(8,128)(2,1)S(1)}, bf16[16,64,256]{2,1,0:T(8,128)(2,1)S(1)}, u32[]{:S(2)}, u32[]{:S(2)}) collective-permute-start(bf16[16,64,256]{2,1,0:T(8,128)(2,1)S(1)} %get-tuple-element.51), channel_id=1, source_target_pairs={{1,0},{2,1},{3,2},{4,3},{5,4},{6,5},{7,6},{8,7},{9,8},{10,9},{11,1... | collective-permute-start | bytes 1572872 | tf_op jit(solution)/shard_map/ppermute | solution.py:274
  21.7 42.7 %collective-permute-start.2 = (bf16[16,64,256]{2,1,0:T(8,128)(2,1)S(1)}, bf16[16,64,256]{2,1,0:T(8,128)(2,1)S(1)}, u32[]{:S(2)}, u32[]{:S(2)}) collective-permute-start(bf16[16,64,256]{2,1,0:T(8,128)(2,1)S(1)} %get-tuple-element.50), channel_id=1, source_target_pairs={{0,1},{1,2},{2,3},{3,4},{4,5},{5,6},{6,7},{7,8},{8,9},{9,10},{10,1... | collective-permute-start | bytes 1572872 | tf_op jit(solution)/shard_map/ppermute | solution.py:273
